TPU v7x, 32 devices: a whole 2x2x4 slice. The times are simulated.
32 devices in a mesh: frames: 8 (over z, y), bins: 4 (over x, core).
Axes of the slice: x: 2, y: 2, z: 4, core: 2. Of those that a mesh axis runs over, the one named last changes fastest.
Arguments:
- spectrum: float32 [16384, 1024], P('frames', 'bins'), may hold values from 0.01 to 4
- sign_bits: int32 [16384], P('frames'), may hold values from 0 to 1
- kept_rows: int32 [4096], replicated, may hold values from 0 to 2047, as said below
- mask: int32 [352, 1024], P(None, 'bins'), may hold values 0 or 1
- w_init: float32 [4096, 352], P('frames'), may hold values from 0.02 to 0.2
- h_init: float32 [352, 1024], P(None, 'bins'), may hold values from 0.02 to 0.2
Outputs:
- activations: float32 [4096, 352], P('frames')
- templates: float32 [352, 1024], P(None, 'bins')
Inputs may be any that keep to these rules, and one draw needn't show every extreme that they name: `kept_rows`: rows i * 512 to (i + 1) * 512 - 1 hold distinct positions, so each block of 2048 frames gives exactly 512 distinct sketch rows.
All inputs are finite; a program needn't handle non-finite values. No bound on the sum of `mask` on one device may be relied on, other than what follows from the above.
Results may differ from a plain program's by a relative error of at most 0.0001.
Values sent between devices are 32-bit elements; how exact they have to be, the bound alone decides.
A program may use at most 64 MiB of HBM per device.

v0:
```python
import jax
import jax.numpy as jnp
from jax import lax
from jax.sharding import PartitionSpec as P

ITERS = 2


def partner_2(value, axis, apart):
    return lax.ppermute(value, axis, [(i, i ^ 1 << apart) for i in range(lax.axis_size(axis))])


def parity_bits(left, right, width):
    joint = jnp.bitwise_and(left, right)
    total = jnp.zeros(joint.shape, jnp.int32)
    for position in range(width):
        total = jnp.bitwise_xor(total, jnp.bitwise_and(jnp.right_shift(joint, position), 1))
    return total


def hadamard(count):
    index = jnp.arange(count, dtype=jnp.int32)
    bits = parity_bits(index[:, None], index[None, :], max(count.bit_length(), 1))
    return (1 - 2 * bits).astype(jnp.float32)


def body(spectrum, sign_bits, kept_rows, mask, w_init, h_init):
    damping = 1.0
    high = lax.Precision.HIGHEST
    block_count = lax.axis_size("frames")
    position = lax.axis_index("frames")
    frame_rows = spectrum.shape[0]
    sketch_rows = kept_rows.shape[0]
    per_block = sketch_rows // block_count
    signed = spectrum * (1 - 2 * sign_bits).astype(jnp.float32)[:, None]
    local = jnp.dot(hadamard(frame_rows), signed, precision=high)
    partial_value = local
    for level in range(block_count.bit_length() - 1):
        partner = partner_2(partial_value, "frames", level)
        upper = jnp.bitwise_and(jnp.right_shift(position, level), 1) == 1
        partial_value = jnp.where(upper, partner - partial_value, partial_value + partner)
    own_rows = lax.dynamic_slice_in_dim(kept_rows, position * per_block, per_block)
    sketch = jnp.take(partial_value, own_rows, axis=0)
    sketch = sketch / jnp.sqrt(jnp.float32(frame_rows * block_count))
    templates = h_init * mask.astype(jnp.float32)
    activations = w_init
    for round_index in range(ITERS):
        gram_h, proj = lax.psum(
            (
                jnp.dot(templates, templates.T, precision=high),
                jnp.dot(sketch, templates.T, precision=high),
            ),
            "bins",
        )
        lower = jnp.maximum(-proj, 0.0) + jnp.dot(activations, gram_h, precision=high) + damping
        activations = activations * jnp.sqrt((jnp.maximum(proj, 0.0) + damping) / lower)
        cross, gram_w = lax.psum(
            (
                jnp.dot(activations.T, sketch, precision=high),
                jnp.dot(activations.T, activations, precision=high),
            ),
            "frames",
        )
        lower = jnp.maximum(-cross, 0.0) + jnp.dot(gram_w, templates, precision=high) + damping
        templates = templates * jnp.sqrt((jnp.maximum(cross, 0.0) + damping) / lower)
    return (activations, templates)


def solution(mesh):
    in_specs = (
        P("frames", "bins"),
        P("frames"),
        P(),
        P(None, "bins"),
        P("frames", None),
        P(None, "bins"),
    )
    out_specs = (P("frames", None), P(None, "bins"))
    return jax.shard_map(body, mesh=mesh, in_specs=in_specs, out_specs=out_specs, check_vma=False)
```

profile of v0, /device:TPU:0, one launch (start us, length us, event | category | flops | bytes accessed | tf_op | source)
XLA Modules:
  0.0 719.4 jit_solution(10122737167420185647)
XLA Ops:
  7.9 254.4 %fusion = f32[2048,256]{1,0:T(8,128)S(1)} fusion(f32[2048,256]{1,0:T(8,128)} %param.6, f32[2048]{0:T(1024)S(1)} %subtract_convert_fusion), kind=kOutput, calls=%fused_computation.1 | convolution fusion | flops 13049004032 | bytes 4202496 | tf_op jit(solution)/shard_map/dot_general | solution.py:36
  262.3 3.0 collective-permute-start
  265.4 45.7 %collective-permute-done = f32[2048,256]{1,0:T(8,128)} collective-permute-done((f32[2048,256]{1,0:T(8,128)S(1)}, f32[2048,256]{1,0:T(8,128)}, u32[]{:S(2)}, u32[]{:S(2)}) %collective-permute-start) | collective-permute-done | bytes 2097184 | tf_op jit(solution)/shard_map/ppermute | solution.py:10
  311.1 2.5 add_select_fusion.2
  313.6 1.9 collective-permute-start.1
  315.5 45.1 %collective-permute-done.1 = f32[2048,256]{1,0:T(8,128)} collective-permute-done((f32[2048,256]{1,0:T(8,128)S(1)}, f32[2048,256]{1,0:T(8,128)}, u32[]{:S(2)}, u32[]{:S(2)}) %collective-permute-start.1) | collective-permute-done | bytes 2097184 | tf_op jit(solution)/shard_map/ppermute | solution.py:10
  360.6 2.5 add_select_fusion.1
  363.1 2.6 collective-permute-start.2
  368.0 87.0 %collective-permute-done.2 = f32[2048,256]{1,0:T(8,128)} collective-permute-done((f32[2048,256]{1,0:T(8,128)S(1)}, f32[2048,256]{1,0:T(8,128)}, u32[]{:S(2)}, u32[]{:S(2)}) %collective-permute-start.2) | collective-permute-done | bytes 2097184 | tf_op jit(solution)/shard_map/ppermute | solution.py:10
  455.0 2.5 add_select_fusion
  459.1 1.8 fusion.76
  460.9 39.4 %all-reduce.15.cloned.1.call-done = (f32[352,352]{1,0:T(8,128)}, f32[512,352]{0,1:T(8,128)}) async-done(((f32[352,352]{1,0:T(8,128)}, f32[512,352]{0,1:T(8,128)}), (f32[352,352]{1,0:T(8,128)}, f32[512,352]{0,1:T(8,128)})) %all-reduce.15.cloned.1.call-update) | async-done | bytes 1216528 | tf_op jit(solution)/shard_map/psum | solution.py:48
  500.4 2.9 fusion.59
  503.3 1.6 fusion.75
  504.9 2.1 fusion.110
  507.1 76.5 %all-reduce.11.cloned.1.call-done = (f32[352,352]{1,0:T(8,128)}, f32[352,256]{1,0:T(8,128)}) async-done(((f32[352,352]{1,0:T(8,128)}, f32[352,256]{1,0:T(8,128)}), (f32[352,352]{1,0:T(8,128)}, f32[352,256]{1,0:T(8,128)})) %all-reduce.11.cloned.1.call-update) | async-done | bytes 856080 | tf_op jit(solution)/shard_map/psum | solution.py:57
  583.6 2.1 fusion.67
  585.7 1.8 fusion.74
  589.2 37.6 %all-reduce.13.cloned.1.call-done = (f32[352,352]{1,0:T(8,128)}, f32[512,352]{0,1:T(8,128)}) async-done(((f32[352,352]{1,0:T(8,128)}, f32[512,352]{0,1:T(8,128)}), (f32[352,352]{1,0:T(8,128)}, f32[512,352]{0,1:T(8,128)})) %all-reduce.13.cloned.1.call-update) | async-done | bytes 1216528 | tf_op jit(solution)/shard_map/psum | solution.py:48
  626.8 3.0 fusion.63
  629.8 1.6 fusion.73
  631.4 2.1 fusion.112
  633.5 76.6 %all-reduce.9.cloned.1.call-done = (f32[352,352]{1,0:T(8,128)}, f32[352,256]{1,0:T(8,128)}) async-done(((f32[352,352]{1,0:T(8,128)}, f32[352,256]{1,0:T(8,128)}), (f32[352,352]{1,0:T(8,128)}, f32[352,256]{1,0:T(8,128)})) %all-reduce.9.cloned.1.call-update) | async-done | bytes 856080 | tf_op jit(solution)/shard_map/psum | solution.py:57
  710.1 2.8 fusion.71
  (28 shorter events, 6.6 us)
Async XLA Ops:
  7.2 493.2 %all-reduce.15.cloned.1.call-start = ((), (), s32[]{:S(2)}) async-start(), calls=%async_computation.3 | async-start | bytes 2523136 | tf_op jit(solution)/shard_map/psum | solution.py:48
  262.3 3.0 copy-start.3
  262.3 48.8 %collective-permute-start = (f32[2048,256]{1,0:T(8,128)S(1)}, f32[2048,256]{1,0:T(8,128)}, u32[]{:S(2)}, u32[]{:S(2)}) collective-permute-start(f32[2048,256]{1,0:T(8,128)S(1)} %fusion), channel_id=1, source_target_pairs={{0,4},{4,0},{8,12},{12,8},{16,20},{20,16},{24,28},{28,24},{1,5},{5... | collective-permute-start | bytes 6291464 | tf_op jit(solution)/shard_map/ppermute | solution.py:10
  313.6 1.9 copy-start.1
  313.6 47.0 %collective-permute-start.1 = (f32[2048,256]{1,0:T(8,128)S(1)}, f32[2048,256]{1,0:T(8,128)}, u32[]{:S(2)}, u32[]{:S(2)}) collective-permute-start(f32[2048,256]{1,0:T(8,128)S(1)} %add_select_fusion.2), channel_id=1, source_target_pairs={{0,8},{4,12},{8,0},{12,4},{16,24},{20,28},{24,16},{28,20},{1,9},{5... | collective-permute-start | bytes 6291464 | tf_op jit(solution)/shard_map/ppermute | solution.py:10
  315.5 51.0 %copy-start.4 = (f32[352,256]{1,0:T(8,128)S(1)}, f32[352,256]{1,0:T(8,128)}, u32[]{:S(2)}) copy-start(f32[352,256]{1,0:T(8,128)} %param.11) | copy-start | bytes 1081348
  315.5 51.0 %copy-start.5 = (s32[352,256]{1,0:T(8,128)S(1)}, s32[352,256]{1,0:T(8,128)}, u32[]{:S(2)}) copy-start(s32[352,256]{1,0:T(8,128)} %param.9) | copy-start | bytes 1081348
  363.1 4.9 copy-start
  363.1 91.9 %collective-permute-start.2 = (f32[2048,256]{1,0:T(8,128)S(1)}, f32[2048,256]{1,0:T(8,128)}, u32[]{:S(2)}, u32[]{:S(2)}) collective-permute-start(f32[2048,256]{1,0:T(8,128)S(1)} %add_select_fusion.1), channel_id=1, source_target_pairs={{0,16},{4,20},{8,24},{12,28},{16,0},{20,4},{24,8},{28,12},{1,17},{... | collective-permute-start | bytes 6291464 | tf_op jit(solution)/shard_map/ppermute | solution.py:10
  459.1 41.3 %copy-start.6 = (f32[512,352]{0,1:T(8,128)S(1)}, f32[512,352]{0,1:T(8,128)}, u32[]{:S(2)}) copy-start(f32[512,352]{0,1:T(8,128)} %param.10) | copy-start | bytes 2162692
  460.9 122.7 %all-reduce.11.cloned.1.call-start = ((), (), s32[]{:S(2)}) async-start(), calls=%async_computation.1 | async-start | bytes 1802240 | tf_op jit(solution)/shard_map/psum | solution.py:57
  507.0 119.8 %all-reduce.13.cloned.1.call-start = ((), (), s32[]{:S(2)}) async-start(), calls=%async_computation.2 | async-start | bytes 2523136 | tf_op jit(solution)/shard_map/psum | solution.py:48
  589.0 121.1 %all-reduce.9.cloned.1.call-start = ((), (), s32[]{:S(2)}) async-start(), calls=%async_computation | async-start | bytes 1802240 | tf_op jit(solution)/shard_map/psum | solution.py:57
  629.8 3.7 copy-start.2
Sparse Core Ops, SparseCore 0:
  461.0 39.2 all-reduce.14
  507.1 76.3 all-reduce.10
  589.1 37.6 all-reduce.12
  633.7 76.4 all-reduce.8
where the time goes:
time: 734 us; the launch traced here: 719 us
  waiting for transfers between devices  408 us (56%)
  matrix products  279 us (38%)
  between operations  13.9 us (2%)
  other arithmetic  8.95 us (1%)
  starting transfers between devices  7.8 us (1%)
    dot_general x1, matrix products, body(): local = jnp.dot(hadamard(frame_rows), signed, precision=high)  254 us
    ppermute x3, waiting for transfers between devices, partner_2(): lax.ppermute(value, axis, [(i, i ^ 1 << apart) for i in range(lax.axis_si...  178 us
    psum x2, waiting for transfers between devices, body(): lax.psum((jnp.dot(activations.T, sketch, precision=high), jnp.dot(activat...  153 us
    psum x2, waiting for transfers between devices, body(): lax.psum((jnp.dot(templates, templates.T, precision=high), jnp.dot(sketch...  77 us
  transfers between devices with their start and end apart: 7, of which 7 were waited for; matrix products, arithmetic and copies ran while one was open for 0% of the time, Pallas kernels for 0%

commit v1 on v0

v1 whole, which is shorter than its diff:
```python
import jax
import jax.numpy as jnp
import numpy as np
from jax import lax
from jax.sharding import PartitionSpec as P

ITERS = 2
SIDE = 256


def hadamard_np(count):
    table = np.ones((1, 1), np.float32)
    while table.shape[0] < count:
        table = np.block([[table, table], [table, -table]])
    return table


def split_2(value):
    high = lax.reduce_precision(value, 8, 7)
    return high.astype(jnp.bfloat16), (value - high).astype(jnp.bfloat16)


def local_hadamard(signed):
    rows, cols = signed.shape
    side = min(SIDE, rows)
    outer = rows // side
    table = jnp.asarray(hadamard_np(side), jnp.bfloat16)
    blocks = signed.reshape(outer, side, cols)
    high, low = split_2(blocks)
    dims = (((1,), (1,)), ((), ()))
    parts = []
    for index in range(outer):
        value = lax.dot_general(table, high[index], (((1,), (0,)), ((), ())), preferred_element_type=jnp.float32)
        value += lax.dot_general(table, low[index], (((1,), (0,)), ((), ())), preferred_element_type=jnp.float32)
        parts.append(value)
    step = 1
    while step < outer:
        nxt = list(parts)
        for index in range(outer):
            if not index & step:
                nxt[index] = parts[index] + parts[index | step]
                nxt[index | step] = parts[index] - parts[index | step]
        parts = nxt
        step *= 2
    return jnp.concatenate(parts, axis=0)


def body(spectrum, sign_bits, kept_rows, mask, w_init, h_init):
    damping = 1.0
    high = lax.Precision.HIGH
    block_count = lax.axis_size("frames")
    position = lax.axis_index("frames")
    frame_rows, cols = spectrum.shape
    per_block = kept_rows.shape[0] // block_count
    signed = spectrum * (1 - 2 * sign_bits).astype(jnp.float32)[:, None]
    local = local_hadamard(signed)
    value = jnp.take(local, kept_rows, axis=0, mode="clip").reshape(block_count, per_block, cols)
    levels = block_count.bit_length() - 1
    for level in range(levels):
        bit = jnp.bitwise_and(jnp.right_shift(position, level), 1)
        pairs = value.reshape(value.shape[0] // 2, 2, per_block, cols)
        keep = lax.dynamic_index_in_dim(pairs, bit, 1, keepdims=False)
        send = lax.dynamic_index_in_dim(pairs, 1 - bit, 1, keepdims=False)
        size = lax.axis_size("frames")
        got = lax.ppermute(send, "frames", [(i, i ^ 1 << level) for i in range(size)])
        value = jnp.where(bit == 1, got - keep, keep + got)
    sketch = value.reshape(per_block, cols)
    sketch = sketch / jnp.sqrt(jnp.float32(frame_rows * block_count))
    templates = h_init * mask.astype(jnp.float32)
    activations = w_init
    for round_index in range(ITERS):
        gram_h, proj = lax.psum(
            (
                jnp.dot(templates, templates.T, precision=high),
                jnp.dot(sketch, templates.T, precision=high),
            ),
            "bins",
        )
        lower = jnp.maximum(-proj, 0.0) + jnp.dot(activations, gram_h, precision=high) + damping
        activations = activations * jnp.sqrt((jnp.maximum(proj, 0.0) + damping) / lower)
        cross, gram_w = lax.psum(
            (
                jnp.dot(activations.T, sketch, precision=high),
                jnp.dot(activations.T, activations, precision=high),
            ),
            "frames",
        )
        lower = jnp.maximum(-cross, 0.0) + jnp.dot(gram_w, templates, precision=high) + damping
        templates = templates * jnp.sqrt((jnp.maximum(cross, 0.0) + damping) / lower)
    return (activations, templates)


def solution(mesh):
    in_specs = (
        P("frames", "bins"),
        P("frames"),
        P(),
        P(None, "bins"),
        P("frames", None),
        P(None, "bins"),
    )
    out_specs = (P("frames", None), P(None, "bins"))
    return jax.shard_map(body, mesh=mesh, in_specs=in_specs, out_specs=out_specs, check_vma=False)
```

time: 734 us -> 391 us (0.53); the launches traced: 719 us -> 390 us
  matrix products: 279 us -> 24.2 us
  waiting for transfers between devices: 408 us -> 318 us
  local copies, waits for them, and re-layouts: 1.61 us -> 18.9 us
    dot_general x1 -> x16, matrix products: 254 us -> 2.99 us  [the longest x8 1.54 us: local_hadamard(): lax.dot_general(table, low[index], (((1,), (0,)), ((), ())), preferred_el...]
    ppermute x3, waiting for transfers between devices: 178 us -> 87.9 us  [body(): lax.ppermute(send, 'frames', [(i, i ^ 1 << level) for i in range(size)])]
    gather x1, local copies, waits for them, and re-layouts: 1.57 us -> 16.1 us  [body(): jnp.take(local, kept_rows, axis=0, mode='clip')]
  transfers between devices with their start and end apart: 7 -> 7, of which waited for: 7 -> 7; matrix products, arithmetic and copies ran while one was open for 0% -> 1% of each run, Pallas kernels for 0% -> 0%
where the time goes in v1:
time: 391 us; the launch traced here: 390 us
  waiting for transfers between devices  318 us (81%)
  matrix products  24.2 us (6%)
  local copies, waits for them, and re-layouts  18.9 us (5%)
  between operations  14.1 us (4%)
  starting transfers between devices  7.6 us (2%)
  other arithmetic  7.52 us (2%)
    psum x2, waiting for transfers between devices, body(): lax.psum((jnp.dot(activations.T, sketch, precision=high), jnp.dot(activat...  153 us
    ppermute x3, waiting for transfers between devices, body(): lax.ppermute(send, 'frames', [(i, i ^ 1 << level) for i in range(size)])  87.9 us
    psum x2, waiting for transfers between devices, body(): lax.psum((jnp.dot(templates, templates.T, precision=high), jnp.dot(sketch...  77.2 us
    gather x1, local copies, waits for them, and re-layouts, body(): jnp.take(local, kept_rows, axis=0, mode='clip')  16.1 us
  transfers between devices with their start and end apart: 7, of which 7 were waited for; matrix products, arithmetic and copies ran while one was open for 1% of the time, Pallas kernels for 0%

profile of v1, /device:TPU:0, one launch (start us, length us, event | category | flops | bytes accessed | tf_op | source)
XLA Modules:
  0.0 390.5 jit_solution(10839885978442829898)
XLA Ops:
  7.9 1.9 broadcast_multiply_fusion
  15.0 16.1 %gather_fusion = f32[4096,256]{1,0:T(8,128)} fusion(f32[2048,256]{1,0:T(8,128)S(1)} %bitcast_dynamic-update-slice_fusion, s32[4096]{0:T(1024)S(1)} %broadcast_clamp_fusion), kind=kCustom, calls=%fused_computation | custom fusion | bytes 8404992 | tf_op jit(solution)/shard_map/jit(_take)/gather | solution.py:57
  31.1 1.7 dynamic-slice_bitcast_fusion
  32.8 3.0 collective-permute-start
  35.8 45.7 %collective-permute-done = f32[4,512,256]{2,1,0:T(8,128)} collective-permute-done((f32[4,512,256]{2,1,0:T(8,128)S(1)}, f32[4,512,256]{2,1,0:T(8,128)}, u32[]{:S(2)}, u32[]{:S(2)}) %collective-permute-start) | collective-permute-done | bytes 2097184 | tf_op jit(solution)/shard_map/ppermute | solution.py:65
  81.6 2.5 fusion.1
  84.1 1.9 collective-permute-start.1
  86.0 22.7 %collective-permute-done.1 = f32[2,512,256]{2,1,0:T(8,128)} collective-permute-done((f32[2,512,256]{2,1,0:T(8,128)S(1)}, f32[2,512,256]{2,1,0:T(8,128)}, u32[]{:S(2)}, u32[]{:S(2)}) %collective-permute-start.1) | collective-permute-done | bytes 1048608 | tf_op jit(solution)/shard_map/ppermute | solution.py:65
  108.7 1.4 fusion.19
  110.1 2.5 collective-permute-start.2
  112.6 2.4 fusion.36
  115.0 19.5 %collective-permute-done.2 = f32[1,512,256]{2,1,0:T(8,128)S(1)} collective-permute-done((f32[1,512,256]{2,1,0:T(8,128)S(1)}, f32[1,512,256]{2,1,0:T(8,128)S(1)}, u32[]{:S(2)}, u32[]{:S(2)}) %collective-permute-start.2) | collective-permute-done | bytes 524320 | tf_op jit(solution)/shard_map/ppermute | solution.py:65
  134.6 1.3 fusion.26
  136.0 39.4 %all-reduce.15.cloned.1.call-done = (f32[352,352]{1,0:T(8,128)}, f32[512,352]{0,1:T(8,128)}) async-done(((f32[352,352]{1,0:T(8,128)}, f32[512,352]{0,1:T(8,128)}), (f32[352,352]{1,0:T(8,128)}, f32[512,352]{0,1:T(8,128)})) %all-reduce.15.cloned.1.call-update) | async-done | bytes 1216528 | tf_op jit(solution)/shard_map/psum | solution.py:72
  175.4 2.9 fusion.6
  179.5 1.5 fusion.37
  181.1 76.5 %all-reduce.11.cloned.1.call-done = (f32[352,352]{1,0:T(8,128)}, f32[352,256]{1,0:T(8,128)}) async-done(((f32[352,352]{1,0:T(8,128)}, f32[352,256]{1,0:T(8,128)}), (f32[352,352]{1,0:T(8,128)}, f32[352,256]{1,0:T(8,128)})) %all-reduce.11.cloned.1.call-update) | async-done | bytes 856080 | tf_op jit(solution)/shard_map/psum | solution.py:81
  257.6 1.7 fusion.14
  259.4 1.3 fusion.22
  262.0 37.8 %all-reduce.13.cloned.1.call-done = (f32[352,352]{1,0:T(8,128)}, f32[512,352]{0,1:T(8,128)}) async-done(((f32[352,352]{1,0:T(8,128)}, f32[512,352]{0,1:T(8,128)}), (f32[352,352]{1,0:T(8,128)}, f32[512,352]{0,1:T(8,128)})) %all-reduce.13.cloned.1.call-update) | async-done | bytes 1216528 | tf_op jit(solution)/shard_map/psum | solution.py:72
  299.8 2.3 fusion.10
  303.4 1.5 fusion.39
  305.0 76.5 %all-reduce.9.cloned.1.call-done = (f32[352,352]{1,0:T(8,128)}, f32[352,256]{1,0:T(8,128)}) async-done(((f32[352,352]{1,0:T(8,128)}, f32[352,256]{1,0:T(8,128)}), (f32[352,352]{1,0:T(8,128)}, f32[352,256]{1,0:T(8,128)})) %all-reduce.9.cloned.1.call-update) | async-done | bytes 856080 | tf_op jit(solution)/shard_map/psum | solution.py:81
  381.5 2.4 fusion.18
  (50 shorter events, 9.7 us)
Async XLA Ops:
  7.2 168.3 %all-reduce.15.cloned.1.call-start = ((), (), s32[]{:S(2)}) async-start(), calls=%async_computation.3 | async-start | bytes 2523136 | tf_op jit(solution)/shard_map/psum | solution.py:72
  9.8 0.9 copy-start
  14.3 0.7 copy-start.4
  32.8 48.8 %collective-permute-start = (f32[4,512,256]{2,1,0:T(8,128)S(1)}, f32[4,512,256]{2,1,0:T(8,128)}, u32[]{:S(2)}, u32[]{:S(2)}) collective-permute-start(f32[4,512,256]{2,1,0:T(8,128)S(1)} %dynamic-slice_bitcast_fusion), channel_id=1, source_target_pairs={{0,4},{4,0},{8,12},{12,8},{16,20},{20,16},{24,28},{28,24},{1,5},{5... | collective-permute-start | bytes 6291464 | tf_op jit(solution)/shard_map/ppermute | solution.py:65
  84.1 24.5 %collective-permute-start.1 = (f32[2,512,256]{2,1,0:T(8,128)S(1)}, f32[2,512,256]{2,1,0:T(8,128)}, u32[]{:S(2)}, u32[]{:S(2)}) collective-permute-start(f32[2,512,256]{2,1,0:T(8,128)S(1)} %dynamic-slice_bitcast_fusion.1), channel_id=1, source_target_pairs={{0,8},{4,12},{8,0},{12,4},{16,24},{20,28},{24,16},{28,20},{1,9},{5... | collective-permute-start | bytes 3145736 | tf_op jit(solution)/shard_map/ppermute | solution.py:65
  86.0 26.6 %copy-start.2 = (f32[352,256]{1,0:T(8,128)S(1)}, f32[352,256]{1,0:T(8,128)}, u32[]{:S(2)}) copy-start(f32[352,256]{1,0:T(8,128)} %param.12) | copy-start | bytes 1081348
  110.0 24.5 %copy-start.3 = (s32[352,256]{1,0:T(8,128)S(1)}, s32[352,256]{1,0:T(8,128)}, u32[]{:S(2)}) copy-start(s32[352,256]{1,0:T(8,128)} %param.10) | copy-start | bytes 1081348
  110.1 24.4 %collective-permute-start.2 = (f32[1,512,256]{2,1,0:T(8,128)S(1)}, f32[1,512,256]{2,1,0:T(8,128)S(1)}, u32[]{:S(2)}, u32[]{:S(2)}) collective-permute-start(f32[1,512,256]{2,1,0:T(8,128)S(1)} %constant_dynamic-slice_fusion), channel_id=1, source_target_pairs={{0,16},{4,20},{8,24},{12,28},{16,0},{20,4},{24,8},{28,12},{1,17},{... | collective-permute-start | bytes 1572872 | tf_op jit(solution)/shard_map/ppermute | solution.py:65
  135.9 121.7 %all-reduce.11.cloned.1.call-start = ((), (), s32[]{:S(2)}) async-start(), calls=%async_computation.1 | async-start | bytes 1802240 | tf_op jit(solution)/shard_map/psum | solution.py:81
  181.0 118.8 %all-reduce.13.cloned.1.call-start = ((), (), s32[]{:S(2)}) async-start(), calls=%async_computation.2 | async-start | bytes 2523136 | tf_op jit(solution)/shard_map/psum | solution.py:72
  262.0 119.5 %all-reduce.9.cloned.1.call-start = ((), (), s32[]{:S(2)}) async-start(), calls=%async_computation | async-start | bytes 1802240 | tf_op jit(solution)/shard_map/psum | solution.py:81
  302.2 2.8 copy-start.1
Sparse Core Ops, SparseCore 0:
  136.1 39.3 all-reduce.14
  181.2 76.3 all-reduce.10
  262.1 37.6 all-reduce.12
  305.1 76.3 all-reduce.8

commit v2 on v1

--- a/solution.py
+++ b/solution.py
@@ -2,6 +2,8 @@
 import jax.numpy as jnp
 import numpy as np
 from jax import lax
+from jax.experimental import pallas as pl
+from jax.experimental.pallas import tpu as pltpu
 from jax.sharding import PartitionSpec as P
 
 ITERS = 2
@@ -90,6 +92,234 @@
     return (activations, templates)
 
 
+MESH = pl.DeviceIdType.MESH
+VMEM = pl.BlockSpec(memory_space=pltpu.VMEM)
+DMA = pltpu.SemaphoreType.DMA
+LIMIT = 48 * 1024 * 1024
+
+
+def flip(index, mask):
+    weight = 1
+    result = index
+    while weight <= mask:
+        if mask & weight:
+            result = result + weight - 2 * weight * lax.rem(index // weight, 2)
+        weight *= 2
+    return result
+
+
+def greet(devices):
+    barrier = pltpu.get_barrier_semaphore()
+    for device in devices:
+        pl.semaphore_signal(barrier, inc=1, device_id=device, device_id_type=MESH)
+    pl.semaphore_wait(barrier, len(devices))
+
+
+def send(src, dst, send_sem, recv_sem, device):
+    copy = pltpu.make_async_remote_copy(
+        src_ref=src, dst_ref=dst, send_sem=send_sem, recv_sem=recv_sem, device_id=device, device_id_type=MESH
+    )
+    copy.start()
+    return copy
+
+
+def sketch_kernel(scale, c_ref, out_ref, got_y, got_z, part, send_sem, recv_sem):
+    me, col = lax.axis_index("frames"), lax.axis_index("bins")
+    side = (flip(me, 1), col)
+    near = (flip(me, 2), col)
+    far = (flip(me, 4), col)
+    greet([side, near, far])
+    copies = {}
+    for z in (3, 2, 1, 0):
+        copies[z] = send(c_ref.at[2 * z + 1], got_y.at[z], send_sem.at[z], recv_sem.at[z], side)
+    copies[3].wait_recv()
+    part[0] = c_ref[6] + got_y[3]
+    first = send(part.at[0], got_z.at[0], send_sem.at[4], recv_sem.at[4], near)
+    copies[2].wait_recv()
+    first.wait_recv()
+    part[1] = c_ref[4] + got_y[2] + got_z[0]
+    second = send(part.at[1], got_z.at[1], send_sem.at[5], recv_sem.at[5], far)
+    copies[1].wait_recv()
+    part[2] = c_ref[2] + got_y[1]
+    third = send(part.at[2], got_z.at[2], send_sem.at[6], recv_sem.at[6], near)
+    copies[0].wait_recv()
+    third.wait_recv()
+    second.wait_recv()
+    out_ref[...] = ((c_ref[0] + got_y[0]) + (got_z[2] + got_z[1])) * scale
+    for copy in (*copies.values(), first, second, third):
+        copy.wait_send()
+
+
+def sum_sketch(terms, scale):
+    _, rows, cols = terms.shape
+    f32 = jnp.float32
+    return pl.pallas_call(
+        lambda *refs: sketch_kernel(scale, *refs),
+        out_shape=jax.ShapeDtypeStruct((rows, cols), f32),
+        in_specs=[VMEM],
+        out_specs=VMEM,
+        scratch_shapes=[
+            pltpu.VMEM((4, rows, cols), f32),
+            pltpu.VMEM((3, rows, cols), f32),
+            pltpu.VMEM((3, rows, cols), f32),
+            DMA((7,)),
+            DMA((7,)),
+        ],
+        compiler_params=pltpu.CompilerParams(collective_id=0, has_side_effects=True, vmem_limit_bytes=LIMIT),
+        name="sum_sketch",
+    )(terms)
+
+
+def bins_kernel(g_ref, p_ref, g_out, p_out, g_core, p_core, g_sum, p_sum, g_chip, p_chip, send_sem, recv_sem):
+    row, me = lax.axis_index("frames"), lax.axis_index("bins")
+    core = lax.rem(me, 2)
+    sibling = (row, flip(me, 1))
+    across = (row, flip(me, 2))
+    greet([sibling, across])
+    g_half, p_half = g_ref.shape[0] // 2, p_ref.shape[0] // 2
+
+    def half(ref, which, size):
+        return ref.at[pl.ds(pl.multiple_of(which * size, 8), size)]
+
+    arrays = ((g_ref, g_out, g_core, g_sum, g_chip, g_half), (p_ref, p_out, p_core, p_sum, p_chip, p_half))
+    stage_1 = [
+        send(half(src, 1 - core, size), got, send_sem.at[k], recv_sem.at[k], sibling)
+        for k, (src, _, got, _, _, size) in enumerate(arrays)
+    ]
+    stage_2 = []
+    for k, (src, _, got, total, chip, size) in enumerate(arrays):
+        stage_1[k].wait_recv()
+        total[...] = half(src, core, size)[...] + got[...]
+        stage_2.append(send(total, chip, send_sem.at[2 + k], recv_sem.at[2 + k], across))
+    stage_3 = []
+    for k, (_, out, _, total, chip, size) in enumerate(arrays):
+        stage_2[k].wait_recv()
+        mine = half(out, core, size)
+        mine[...] = total[...] + chip[...]
+        stage_3.append(send(mine, mine, send_sem.at[4 + k], recv_sem.at[4 + k], sibling))
+    for copy in stage_3:
+        copy.wait_recv()
+    for copy in (*stage_1, *stage_2, *stage_3):
+        copy.wait_send()
+
+
+def sum_bins(gram, proj):
+    f32 = jnp.float32
+    g_half = (gram.shape[0] // 2, gram.shape[1])
+    p_half = (proj.shape[0] // 2, proj.shape[1])
+    return pl.pallas_call(
+        bins_kernel,
+        out_shape=(jax.ShapeDtypeStruct(gram.shape, f32), jax.ShapeDtypeStruct(proj.shape, f32)),
+        in_specs=[VMEM, VMEM],
+        out_specs=(VMEM, VMEM),
+        scratch_shapes=[pltpu.VMEM(shape, f32) for _ in range(3) for shape in (g_half, p_half)] + [DMA((6,)), DMA((6,))],
+        compiler_params=pltpu.CompilerParams(collective_id=1, has_side_effects=True, vmem_limit_bytes=LIMIT),
+        name="sum_bins",
+    )(gram, proj)
+
+
+def frames_kernel(g_ref, c_ref, g_out, c_out, g_got, c_got, send_sem, recv_sem):
+    me, col = lax.axis_index("frames"), lax.axis_index("bins")
+    others = [7, 6, 5, 4, 3, 2, 1]
+    device = {r: (flip(me, r), col) for r in others}
+    sibling = (me, flip(col, 1))
+    across = (me, flip(col, 2))
+    greet([device[r] for r in others] + [sibling, across])
+    copies = []
+    for r in others:
+        copies.append(send(g_ref.at[flip(me, r)], g_got.at[r], send_sem.at[r], recv_sem.at[r], device[r]))
+    for r in others:
+        copies.append(send(c_ref.at[flip(me, r)], c_got.at[r], send_sem.at[8 + r], recv_sem.at[8 + r], device[r]))
+    for copy in copies[:7]:
+        copy.wait_recv()
+    total = g_ref[me]
+    for r in others:
+        total = total + g_got[r]
+    g_out[col, me] = total
+    mine = g_out.at[col, me]
+    g_copies = [send(mine, mine, send_sem.at[16 + r], recv_sem.at[16 + r], device[r]) for r in others]
+    for copy in copies[7:]:
+        copy.wait_recv()
+    total = c_ref[me]
+    for r in others:
+        total = total + c_got[r]
+    c_out[me] = total
+    mine = c_out.at[me]
+    c_copies = [send(mine, mine, send_sem.at[24 + r], recv_sem.at[24 + r], device[r]) for r in others]
+    for copy in g_copies:
+        copy.wait_recv()
+    mine = g_out.at[col]
+    to_chip = send(mine, mine, send_sem.at[0], recv_sem.at[0], across)
+    to_core = send(mine, mine, send_sem.at[8], recv_sem.at[8], sibling)
+    to_chip.wait_recv()
+    theirs = g_out.at[flip(col, 2)]
+    passed = send(theirs, theirs, send_sem.at[16], recv_sem.at[16], sibling)
+    for copy in (to_core, passed, *c_copies):
+        copy.wait_recv()
+    for copy in (*copies, *g_copies, *c_copies, to_chip, to_core, passed):
+        copy.wait_send()
+
+
+def sum_frames(gram, cross):
+    f32 = jnp.float32
+    return pl.pallas_call(
+        frames_kernel,
+        out_shape=(jax.ShapeDtypeStruct((4, *gram.shape), f32), jax.ShapeDtypeStruct(cross.shape, f32)),
+        in_specs=[VMEM, VMEM],
+        out_specs=(VMEM, VMEM),
+        scratch_shapes=[pltpu.VMEM(gram.shape, f32), pltpu.VMEM(cross.shape, f32), DMA((32,)), DMA((32,))],
+        compiler_params=pltpu.CompilerParams(collective_id=2, has_side_effects=True, vmem_limit_bytes=LIMIT),
+        name="sum_frames",
+    )(gram, cross)
+
+
+def body_8x4(spectrum, sign_bits, kept_rows, mask, w_init, h_init):
+    damping = 1.0
+    high = lax.Precision.HIGH
+    block_count = 8
+    position = lax.axis_index("frames")
+    column = lax.axis_index("bins")
+    frame_rows, cols = spectrum.shape
+    per_block = kept_rows.shape[0] // block_count
+    parts = w_init.shape[1]
+    signed = spectrum * (1 - 2 * sign_bits).astype(jnp.float32)[:, None]
+    local = local_hadamard(signed)
+    blocks = jnp.bitwise_xor(position, jnp.arange(block_count, dtype=jnp.int32))
+    rows = jnp.take(kept_rows.reshape(block_count, per_block), blocks, axis=0, mode="clip")
+    odd = parity_bits(position, blocks, 3)
+    signs = (1 - 2 * odd).astype(jnp.float32)[:, None, None]
+    terms = jnp.take(local, rows.reshape(-1), axis=0, mode="clip").reshape(block_count, per_block, cols) * signs
+    sketch = sum_sketch(terms, 1.0 / (frame_rows * block_count) ** 0.5)
+    templates = h_init * mask.astype(jnp.float32)
+    activations = w_init
+    quarter = parts // 4
+    for round_index in range(ITERS):
+        gram_h, proj = sum_bins(
+            jnp.dot(templates, templates.T, precision=high),
+            jnp.dot(sketch, templates.T, precision=high),
+        )
+        lower = jnp.maximum(-proj, 0.0) + jnp.dot(activations, gram_h, precision=high) + damping
+        activations = activations * jnp.sqrt((jnp.maximum(proj, 0.0) + damping) / lower)
+        own = lax.dynamic_slice_in_dim(activations, column * quarter, quarter, axis=1)
+        gram_w, cross = sum_frames(
+            jnp.dot(own.T, activations, precision=high).reshape(8, quarter // 8, parts),
+            jnp.dot(activations.T, sketch, precision=high).reshape(8, parts // 8, cols),
+        )
+        gram_w = gram_w.reshape(parts, parts)
+        cross = cross.reshape(parts, cols)
+        lower = jnp.maximum(-cross, 0.0) + jnp.dot(gram_w, templates, precision=high) + damping
+        templates = templates * jnp.sqrt((jnp.maximum(cross, 0.0) + damping) / lower)
+    return (activations, templates)
+
+
+def parity_bits(left, right, width):
+    joint = jnp.bitwise_and(left, right)
+    total = jnp.zeros(joint.shape, jnp.int32)
+    for place in range(width):
+        total = jnp.bitwise_xor(total, jnp.bitwise_and(jnp.right_shift(joint, place), 1))
+    return total
+
+
 def solution(mesh):
     in_specs = (
         P("frames", "bins"),
@@ -100,4 +330,5 @@
         P(None, "bins"),
     )
     out_specs = (P("frames", None), P(None, "bins"))
-    return jax.shard_map(body, mesh=mesh, in_specs=in_specs, out_specs=out_specs, check_vma=False)
+    small = mesh.shape["frames"] == 8 and mesh.shape["bins"] == 4
+    return jax.shard_map(body_8x4 if small else body, mesh=mesh, in_specs=in_specs, out_specs=out_specs, check_vma=False)

time: 391 us -> 216 us (0.55)
  waiting for transfers between devices: 318 us -> 0 us
  Pallas kernels: 0 us -> 167 us
  between operations: 14.1 us -> 1.1 us
  matrix products: 24.2 us -> 14.5 us
  starting transfers between devices: 7.6 us -> 0 us
  local copies, waits for them, and re-layouts: 18.9 us -> 24.9 us
    psum x4 -> x0, waiting for transfers between devices: 230 us -> none  [the longest x2 153 us: body(): lax.psum((jnp.dot(activations.T, sketch, precision=high), jnp.dot(activat...]
    pallas_call x0 -> x5, Pallas kernels: none -> 167 us  [the longest x1 63.8 us: sum_sketch(): pl.pallas_call(lambda *refs: sketch_kernel(scale, *refs), out_shape=jax.S...]
    ppermute x3 -> x0, waiting for transfers between devices: 87.9 us -> none  [body(): lax.ppermute(send, 'frames', [(i, i ^ 1 << level) for i in range(size)])]
    dot_general x12, matrix products: 21.2 us -> 11.5 us  [the longest x2 3.78 us: body_8x4(): jnp.dot(activations, gram_h, precision=high)]
    ppermute x3 -> x0, starting transfers between devices: 7.44 us -> none  [body(): lax.ppermute(send, 'frames', [(i, i ^ 1 << level) for i in range(size)])]
    gather x1 -> x2, local copies, waits for them, and re-layouts: 16.1 us -> 16.9 us  [the longest x1 16.3 us: body_8x4(): jnp.take(local, rows.reshape(-1), axis=0, mode='clip')]
  transfers between devices with their start and end apart: 7 -> 0, of which waited for: 7 -> 0; matrix products, arithmetic and copies ran while one was open for 1% -> 0% of each run, Pallas kernels for 0% -> 0%
where the time goes in v2:
time: 216 us; the launch traced here: 215 us
  Pallas kernels  167 us (77%)
  local copies, waits for them, and re-layouts  24.9 us (12%)
  matrix products  14.5 us (7%)
  other arithmetic  7.22 us (3%)
    pallas_call x1, Pallas kernels, sum_sketch(): pl.pallas_call(lambda *refs: sketch_kernel(scale, *refs), out_shape=jax.S...  63.8 us
    pallas_call x2, Pallas kernels, sum_frames(): pl.pallas_call(frames_kernel, out_shape=(jax.ShapeDtypeStruct((4, *gram.s...  63.2 us
    pallas_call x2, Pallas kernels, sum_bins(): pl.pallas_call(bins_kernel, out_shape=(jax.ShapeDtypeStruct(gram.shape, f...  40.4 us
    gather x1, local copies, waits for them, and re-layouts, body_8x4(): jnp.take(local, rows.reshape(-1), axis=0, mode='clip')  16.3 us
    unnamed x11, local copies, waits for them, and re-layouts  4.35 us

profile of v2, /device:TPU:0, one launch (start us, length us, event | category | flops | bytes accessed | tf_op | source)
XLA Modules:
  0.0 215.1 jit_solution(17017689865898350905)
XLA Ops:
  0.6 0.7 subtract_convert_fusion
  1.3 1.9 broadcast_multiply_fusion.1
  8.4 0.6 gather_fusion
  9.0 16.3 %gather_fusion.1 = f32[4096,256]{1,0:T(8,128)} fusion(f32[2048,256]{1,0:T(8,128)S(1)} %bitcast_dynamic-update-slice_fusion, s32[4096]{0:T(1024)S(1)} %broadcast_clamp_fusion), kind=kCustom, calls=%fused_computation.1 | custom fusion | bytes 8404992 | tf_op jit(solution)/shard_map/jit(_take)/gather | solution.py:291
  25.3 2.7 %broadcast_multiply_fusion.refs_0_ = f32[8,512,256]{2,1,0:T(8,128)S(1)} fusion(f32[8,512,256]{2,1,0:T(8,128)} %bitcast.118, f32[8]{0:T(128)S(1)} %subtract_convert_fusion.1), kind=kLoop, calls=%fused_computation.5 | loop fusion | flops 1048576 | bytes 8388640 | tf_op jit(solution)/shard_map/mul | solution.py:291
  28.0 63.8 %sum_sketch.1 = f32[512,256]{1,0:T(8,128)S(1)} custom-call(f32[8,512,256]{2,1,0:T(8,128)S(1)} %broadcast_multiply_fusion.refs_0_), custom_call_target="tpu_custom_call" | custom-call | tf_op jit(solution)/shard_map/sum_sketch/pallas_call | solution.py:156
  91.8 0.6 fusion.32.p_ref
  92.9 20.2 %sum_bins.2 = (f32[352,352]{1,0:T(8,128)S(1)}, f32[512,352]{1,0:T(8,128)S(1)}) custom-call(f32[352,352]{1,0:T(8,128)S(1)} %fusion.33.g_ref, f32[512,352]{1,0:T(8,128)S(1)} %fusion.32.p_ref), custom_call_target="tpu_custom_call" | custom-call | tf_op jit(solution)/shard_map/sum_bins/pallas_call | solution.py:210
  113.1 2.3 %copy.17 = f32[512,352]{1,0:T(8,128)} copy(f32[512,352]{0,1:T(8,128)} %param.11) | data formatting | bytes 1441792 | tf_op args[4]
  115.3 2.6 %fusion.5 = f32[512,352]{1,0:T(8,128)S(1)} fusion(f32[512,352]{1,0:T(8,128)} %copy.17, f32[352,352]{1,0:T(8,128)S(1)} %get-tuple-element.11, f32[512,352]{0,1:T(8,128)} %param.11, f32[512,352]{1,0:T(8,128)S(1)} %get-tuple-element.10), kind=kOutput, calls=%fused_computation.11 | convolution fusion | flops 382074880 | bytes 3379200 | tf_op jit(solution)/shard_map/dot_general | solution.py:301
  118.0 0.8 fusion.34
  119.4 31.3 %sum_frames.2 = (f32[4,8,11,352]{3,2,1,0:T(8,128)S(1)}, f32[8,44,256]{2,1,0:T(8,128)S(1)}) custom-call(f32[8,11,352]{2,1,0:T(8,128)S(1)} %reshape.76.g_ref, f32[8,44,256]{2,1,0:T(8,128)S(1)} %reshape.77.c_ref), custom_call_target="tpu_custom_call" | custom-call | tf_op jit(solution)/shard_map/sum_frames/pallas_call | solution.py:265
  150.7 0.8 negate_maximum_fusion.1
  151.5 1.8 add.163
  153.3 0.8 max.36
  154.0 0.9 reshape.78
  154.9 1.8 fusion.13
  156.8 0.6 fusion.36.p_ref
  157.8 20.2 %sum_bins.3 = (f32[352,352]{1,0:T(8,128)S(1)}, f32[512,352]{1,0:T(8,128)S(1)}) custom-call(f32[352,352]{1,0:T(8,128)S(1)} %fusion.35.g_ref, f32[512,352]{1,0:T(8,128)S(1)} %fusion.36.p_ref), custom_call_target="tpu_custom_call" | custom-call | tf_op jit(solution)/shard_map/sum_bins/pallas_call | solution.py:210
  178.0 1.2 fusion.9
  179.2 0.8 fusion.37
  180.6 31.9 %sum_frames.3 = (f32[4,8,11,352]{3,2,1,0:T(8,128)S(1)}, f32[8,44,256]{2,1,0:T(8,128)S(1)}) custom-call(f32[8,11,352]{2,1,0:T(8,128)S(1)} %reshape.79.g_ref, f32[8,44,256]{2,1,0:T(8,128)S(1)} %reshape.80.c_ref), custom_call_target="tpu_custom_call" | custom-call | tf_op jit(solution)/shard_map/sum_frames/pallas_call | solution.py:265
  212.7 1.3 fusion.17
  214.0 1.1 copy.20
  (50 shorter events, 7.2 us)
Async XLA Ops:
  3.3 0.9 copy-start
  7.7 0.7 copy-start.3
  28.0 63.8 %copy-start.1 = (f32[352,256]{1,0:T(8,128)S(1)}, f32[352,256]{1,0:T(8,128)}, u32[]{:S(2)}) copy-start(f32[352,256]{1,0:T(8,128)} %param.12) | copy-start | bytes 1081348
  28.0 63.8 %copy-start.2 = (s32[352,256]{1,0:T(8,128)S(1)}, s32[352,256]{1,0:T(8,128)}, u32[]{:S(2)}) copy-start(s32[352,256]{1,0:T(8,128)} %param.10) | copy-start | bytes 1081348

commit v3 on v1

--- a/solution.py
+++ b/solution.py
@@ -2,6 +2,8 @@
 import jax.numpy as jnp
 import numpy as np
 from jax import lax
+from jax.experimental import pallas as pl
+from jax.experimental.pallas import tpu as pltpu
 from jax.sharding import PartitionSpec as P
 
 ITERS = 2
@@ -90,6 +92,329 @@
     return (activations, templates)
 
 
+MESH = pl.DeviceIdType.MESH
+VMEM = pl.BlockSpec(memory_space=pltpu.VMEM)
+DMA = pltpu.SemaphoreType.DMA
+LIMIT = 48 * 1024 * 1024
+
+
+def flip(index, mask):
+    weight = 1
+    result = index
+    while weight <= mask:
+        if mask & weight:
+            result = result + weight - 2 * weight * lax.rem(index // weight, 2)
+        weight *= 2
+    return result
+
+
+def greet(devices):
+    barrier = pltpu.get_barrier_semaphore()
+    for device in devices:
+        pl.semaphore_signal(barrier, inc=1, device_id=device, device_id_type=MESH)
+    pl.semaphore_wait(barrier, len(devices))
+
+
+def send(src, dst, send_sem, recv_sem, device):
+    copy = pltpu.make_async_remote_copy(
+        src_ref=src, dst_ref=dst, send_sem=send_sem, recv_sem=recv_sem, device_id=device, device_id_type=MESH
+    )
+    copy.start()
+    return copy
+
+
+def piece(ref, index, size, base=0):
+    return ref.at[pl.ds(pl.multiple_of(base + index * size, 8), size)]
+
+
+def fold(bits, width):
+    while width > 1:
+        width //= 2
+        bits = jnp.bitwise_xor(bits, jnp.right_shift(bits, width))
+    return jnp.bitwise_and(bits, 1)
+
+
+def sketch_kernel(
+    scale, x_ref, s_ref, k_ref, g_ref, out_ref, g_out,
+    term, high, low, rows_ref, got_y, got_z, part, g_core, g_sum, g_chip, send_sem, recv_sem,
+):
+    me, col = lax.axis_index("frames"), lax.axis_index("bins")
+    core = lax.rem(col, 2)
+    side = (flip(me, 1), col)
+    near = (flip(me, 2), col)
+    far = (flip(me, 4), col)
+    sibling = (me, flip(col, 1))
+    across = (me, flip(col, 2))
+    greet([side, near, far, sibling, across])
+    half = g_ref.shape[0] // 2
+    gram_1 = send(piece(g_ref, 1 - core, half), g_core, send_sem.at[7], recv_sem.at[7], sibling)
+    frame_rows = x_ref.shape[0]
+    outer = frame_rows // SIDE
+    tile = 128
+    value = x_ref[...]
+    rounded = value.astype(jnp.bfloat16)
+    high[...] = rounded
+    low[...] = (value - rounded.astype(jnp.float32)).astype(jnp.bfloat16)
+
+    def compute(r):
+        odd = 0
+        for bit in range(3):
+            if not r >> bit & 1:
+                odd = odd + lax.rem(me // (1 << bit), 2)
+
+        def step(index, carry):
+            where = pl.ds(pl.multiple_of(index * tile, tile), tile)
+            kept = k_ref[where, r : r + 1]
+            lane = lax.broadcasted_iota(jnp.int32, (tile, SIDE), 1)
+            bits = fold(jnp.bitwise_and(kept, lane), SIDE.bit_length() - 1)
+            table = (1 - 2 * jnp.bitwise_and(bits + odd, 1)).astype(jnp.float32)
+            upper = jnp.right_shift(kept, 8)
+            for a in range(outer):
+                sign = (1 - 2 * fold(jnp.bitwise_and(upper, a), 8)).astype(jnp.float32)
+                cols = slice(a * SIDE, (a + 1) * SIDE)
+                flips = (1 - 2 * s_ref[:, cols]).astype(jnp.float32)
+                rows_ref[:, cols] = ((table * sign) * flips).astype(jnp.bfloat16)
+            rows = rows_ref[...]
+            term[r, where] = jnp.dot(rows, high[...], preferred_element_type=jnp.float32) + jnp.dot(
+                rows, low[...], preferred_element_type=jnp.float32
+            )
+            return carry
+
+        lax.fori_loop(0, k_ref.shape[0] // tile, step, 0)
+
+    copies = {}
+    for z in (3, 2, 1, 0):
+        compute(2 * z + 1)
+        copies[z] = send(term.at[2 * z + 1], got_y.at[z], send_sem.at[z], recv_sem.at[z], side)
+        if z == 3:
+            gram_1.wait_recv()
+            g_sum[...] = piece(g_ref, core, half)[...] + g_core[...]
+            gram_2 = send(g_sum, g_chip, send_sem.at[8], recv_sem.at[8], across)
+    compute(6)
+    copies[3].wait_recv()
+    part[0] = term[6] + got_y[3]
+    first = send(part.at[0], got_z.at[0], send_sem.at[4], recv_sem.at[4], near)
+    compute(4)
+    gram_2.wait_recv()
+    mine = piece(g_out, core, half)
+    mine[...] = g_sum[...] + g_chip[...]
+    gram_3 = send(mine, mine, send_sem.at[9], recv_sem.at[9], sibling)
+    compute(2)
+    copies[2].wait_recv()
+    first.wait_recv()
+    part[1] = term[4] + got_y[2] + got_z[0]
+    second = send(part.at[1], got_z.at[1], send_sem.at[5], recv_sem.at[5], far)
+    compute(0)
+    copies[1].wait_recv()
+    part[2] = term[2] + got_y[1]
+    third = send(part.at[2], got_z.at[2], send_sem.at[6], recv_sem.at[6], near)
+    copies[0].wait_recv()
+    third.wait_recv()
+    second.wait_recv()
+    out_ref[...] = ((term[0] + got_y[0]) + (got_z[2] + got_z[1])) * scale
+    gram_3.wait_recv()
+    for copy in (*copies.values(), first, second, third, gram_1, gram_2, gram_3):
+        copy.wait_send()
+
+
+def make_sketch(spectrum, sign_row, kept, gram, scale):
+    frame_rows, cols = spectrum.shape
+    rows = kept.shape[0]
+    half = (gram.shape[0] // 2, gram.shape[1])
+    f32, bf16 = jnp.float32, jnp.bfloat16
+    return pl.pallas_call(
+        lambda *refs: sketch_kernel(scale, *refs),
+        out_shape=(jax.ShapeDtypeStruct((rows, cols), f32), jax.ShapeDtypeStruct(gram.shape, f32)),
+        in_specs=[VMEM] * 4,
+        out_specs=(VMEM, VMEM),
+        scratch_shapes=[
+            pltpu.VMEM((8, rows, cols), f32),
+            pltpu.VMEM((frame_rows, cols), bf16),
+            pltpu.VMEM((frame_rows, cols), bf16),
+            pltpu.VMEM((128, frame_rows), bf16),
+            pltpu.VMEM((4, rows, cols), f32),
+            pltpu.VMEM((3, rows, cols), f32),
+            pltpu.VMEM((3, rows, cols), f32),
+            pltpu.VMEM(half, f32),
+            pltpu.VMEM(half, f32),
+            pltpu.VMEM(half, f32),
+            DMA((10,)),
+            DMA((10,)),
+        ],
+        compiler_params=pltpu.CompilerParams(collective_id=0, has_side_effects=True, vmem_limit_bytes=LIMIT),
+        name="make_sketch",
+    )(spectrum, sign_row, kept, gram)
+
+
+def bins_kernel(count, *refs):
+    ins, outs = refs[:count], refs[count : 2 * count]
+    from_core, sums, from_chip = (refs[(2 + i) * count : (3 + i) * count] for i in range(3))
+    send_sem, recv_sem = refs[5 * count :]
+    row, me = lax.axis_index("frames"), lax.axis_index("bins")
+    core = lax.rem(me, 2)
+    sibling = (row, flip(me, 1))
+    across = (row, flip(me, 2))
+    greet([sibling, across])
+    cuts = []
+    for k in range(count):
+        half = ins[k].shape[0] // 2
+        size = half // 2
+        for part in range(2):
+            cuts.append((k, half, part * size, size))
+    stage_1, stage_2, stage_3 = [], [], []
+    for n, (k, half, start, size) in enumerate(cuts):
+        theirs = ins[k].at[pl.ds(pl.multiple_of((1 - core) * half + start, 8), size)]
+        got = from_core[k].at[pl.ds(start, size)]
+        stage_1.append(send(theirs, got, send_sem.at[n], recv_sem.at[n], sibling))
+    for n, (k, half, start, size) in enumerate(cuts):
+        stage_1[n].wait_recv()
+        here = pl.ds(start, size)
+        sums[k][here] = ins[k][pl.ds(pl.multiple_of(core * half + start, 8), size)] + from_core[k][here]
+        stage_2.append(send(sums[k].at[here], from_chip[k].at[here], send_sem.at[8 + n], recv_sem.at[8 + n], across))
+    for n, (k, half, start, size) in enumerate(cuts):
+        stage_2[n].wait_recv()
+        here = pl.ds(start, size)
+        mine = outs[k].at[pl.ds(pl.multiple_of(core * half + start, 8), size)]
+        mine[...] = sums[k][here] + from_chip[k][here]
+        stage_3.append(send(mine, mine, send_sem.at[16 + n], recv_sem.at[16 + n], sibling))
+    for copy in stage_3:
+        copy.wait_recv()
+    for copy in (*stage_1, *stage_2, *stage_3):
+        copy.wait_send()
+
+
+def sum_bins(name, collective_id, *arrays):
+    f32 = jnp.float32
+    count = len(arrays)
+    halves = [(array.shape[0] // 2, array.shape[1]) for array in arrays]
+    return pl.pallas_call(
+        lambda *refs: bins_kernel(count, *refs),
+        out_shape=tuple(jax.ShapeDtypeStruct(array.shape, f32) for array in arrays),
+        in_specs=[VMEM] * count,
+        out_specs=(VMEM,) * count,
+        scratch_shapes=[pltpu.VMEM(shape, f32) for _ in range(3) for shape in halves] + [DMA((24,)), DMA((24,))],
+        compiler_params=pltpu.CompilerParams(collective_id=collective_id, has_side_effects=True, vmem_limit_bytes=LIMIT),
+        name=name,
+    )(*arrays)
+
+
+def frames_kernel(g_ref, c_ref, g_out, c_out, g_y, c_y, g_z, c_z, g_part, c_part, send_sem, recv_sem):
+    me, col = lax.axis_index("frames"), lax.axis_index("bins")
+    core = lax.rem(col, 2)
+    side = (flip(me, 1), col)
+    peers = {z: (flip(me, 2 * z), col) for z in (3, 2, 1)}
+    sibling = (me, flip(col, 1))
+    greet([side, *peers.values(), sibling])
+    g_half = g_ref.shape[0]
+    arrays = (
+        (0, g_ref, g_half // 8, g_y, g_z, g_part, g_out, core * g_half),
+        (16, c_ref, c_ref.shape[0] // 8, c_y, c_z, c_part, c_out, 0),
+    )
+    copies = []
+
+    def go(src, dst, n, device):
+        copies.append(send(src, dst, send_sem.at[n], recv_sem.at[n], device))
+        return copies[-1]
+
+    by_y, by_z, back, passed = {}, {}, {}, {}
+    for k, src, size, from_y, from_z, part, out, base in arrays:
+        for z in (3, 2, 1, 0):
+            by_y[k, z] = go(piece(src, flip(me, 2 * z + 1), size), from_y.at[z], k + z, side)
+    for k, src, size, from_y, from_z, part, out, base in arrays:
+        for z in (3, 2, 1):
+            by_y[k, z].wait_recv()
+            part[z - 1] = piece(src, flip(me, 2 * z), size)[...] + from_y[z]
+            by_z[k, z] = go(part.at[z - 1], from_z.at[z - 1], k + 4 + z, peers[z])
+    for k, src, size, from_y, from_z, part, out, base in arrays:
+        by_y[k, 0].wait_recv()
+        total = piece(src, me, size)[...] + from_y[0]
+        for z in (1, 2, 3):
+            by_z[k, z].wait_recv()
+            total = total + from_z[z - 1]
+        mine = piece(out, me, size, base)
+        mine[...] = total
+        for z in (3, 2, 1):
+            back[k, z] = go(mine, mine, k + 8 + z, peers[z])
+        back[k, 0] = go(mine, mine, k + 8, side)
+    for k, src, size, from_y, from_z, part, out, base in arrays:
+        for z in (1, 2, 3):
+            back[k, z].wait_recv()
+            theirs = piece(out, flip(me, 2 * z), size, base)
+            passed[k, z] = go(theirs, theirs, k + 12 + z, side)
+        if k == 0:
+            back[k, 0].wait_recv()
+            for z in (1, 2, 3):
+                passed[k, z].wait_recv()
+            mine = piece(g_out, core, g_half)
+            swap = go(mine, mine, 12, sibling)
+    back[16, 0].wait_recv()
+    for z in (1, 2, 3):
+        passed[16, z].wait_recv()
+    swap.wait_recv()
+    for copy in copies:
+        copy.wait_send()
+
+
+def sum_frames(gram_half, cross):
+    f32 = jnp.float32
+    parts, cols = cross.shape
+    g_piece = (gram_half.shape[0] // 8, gram_half.shape[1])
+    c_piece = (parts // 8, cols)
+    return pl.pallas_call(
+        frames_kernel,
+        out_shape=(
+            jax.ShapeDtypeStruct((2 * gram_half.shape[0], gram_half.shape[1]), f32),
+            jax.ShapeDtypeStruct(cross.shape, f32),
+        ),
+        in_specs=[VMEM, VMEM],
+        out_specs=(VMEM, VMEM),
+        scratch_shapes=[pltpu.VMEM((count, *shape), f32) for count in (4, 3, 3) for shape in (g_piece, c_piece)]
+        + [DMA((32,)), DMA((32,))],
+        compiler_params=pltpu.CompilerParams(collective_id=2, has_side_effects=True, vmem_limit_bytes=LIMIT),
+        name="sum_frames",
+    )(gram_half, cross)
+
+
+def body_8x4(spectrum, sign_bits, kept_rows, mask, w_init, h_init):
+    damping = 1.0
+    high = lax.Precision.HIGH
+    block_count = 8
+    position = lax.axis_index("frames")
+    core = lax.rem(lax.axis_index("bins"), 2)
+    frame_rows, cols = spectrum.shape
+    per_block = kept_rows.shape[0] // block_count
+    parts = w_init.shape[1]
+    padded = -(-parts // 128) * 128
+    templates = jnp.pad(h_init * mask.astype(jnp.float32), ((0, padded - parts), (0, 0)))
+    activations = jnp.pad(w_init, ((0, 0), (0, padded - parts)))
+    blocks = jnp.bitwise_xor(position, jnp.arange(block_count, dtype=jnp.int32))
+    kept = jnp.take(kept_rows.reshape(block_count, per_block), blocks, axis=0, mode="clip").T
+    sketch, gram_h = make_sketch(
+        spectrum,
+        sign_bits.reshape(1, frame_rows),
+        kept,
+        jnp.dot(templates, templates.T, precision=high),
+        1.0 / (frame_rows * block_count) ** 0.5,
+    )
+    half = padded // 2
+    for round_index in range(ITERS):
+        proj = jnp.dot(sketch, templates.T, precision=high)
+        if round_index == 0:
+            (proj,) = sum_bins("sum_proj", 1, proj)
+        else:
+            gram_h, proj = sum_bins("sum_both", 3, jnp.dot(templates, templates.T, precision=high), proj)
+        lower = jnp.maximum(-proj, 0.0) + jnp.dot(activations, gram_h, precision=high) + damping
+        activations = activations * jnp.sqrt((jnp.maximum(proj, 0.0) + damping) / lower)
+        own = lax.dynamic_slice_in_dim(activations, core * half, half, axis=1)
+        gram_w, cross = sum_frames(
+            jnp.dot(own.T, activations, precision=high),
+            jnp.dot(activations.T, sketch, precision=high),
+        )
+        lower = jnp.maximum(-cross, 0.0) + jnp.dot(gram_w, templates, precision=high) + damping
+        templates = templates * jnp.sqrt((jnp.maximum(cross, 0.0) + damping) / lower)
+    return (activations[:, :parts], templates[:parts])
+
+
 def solution(mesh):
     in_specs = (
         P("frames", "bins"),
@@ -100,4 +425,5 @@
         P(None, "bins"),
     )
     out_specs = (P("frames", None), P(None, "bins"))
-    return jax.shard_map(body, mesh=mesh, in_specs=in_specs, out_specs=out_specs, check_vma=False)
+    small = mesh.shape["frames"] == 8 and mesh.shape["bins"] == 4
+    return jax.shard_map(body_8x4 if small else body, mesh=mesh, in_specs=in_specs, out_specs=out_specs, check_vma=False)

time: 391 us -> 170 us (0.43)
  waiting for transfers between devices: 318 us -> 0 us
  Pallas kernels: 0 us -> 155 us
  local copies, waits for them, and re-layouts: 18.9 us -> 2.96 us
  matrix products: 24.2 us -> 8.74 us
  between operations: 14.1 us -> 0.88 us
  starting transfers between devices: 7.6 us -> 0 us
  other arithmetic: 7.52 us -> 2.11 us
    psum x4 -> x0, waiting for transfers between devices: 230 us -> none  [the longest x2 153 us: body(): lax.psum((jnp.dot(activations.T, sketch, precision=high), jnp.dot(activat...]
    pallas_call x0 -> x5, Pallas kernels: none -> 155 us  [the longest x1 65.6 us: make_sketch(): pl.pallas_call(lambda *refs: sketch_kernel(scale, *refs), out_shape=(jax....]
    ppermute x3 -> x0, waiting for transfers between devices: 87.9 us -> none  [body(): lax.ppermute(send, 'frames', [(i, i ^ 1 << level) for i in range(size)])]
    dot_general x28 -> x12, matrix products: 24.2 us -> 8.74 us  [the longest x2 2.36 us: body_8x4(): jnp.dot(activations, gram_h, precision=high)]
    gather x1 -> x2, local copies, waits for them, and re-layouts: 16.1 us -> 0.68 us  [body_8x4(): jnp.take(kept_rows.reshape(block_count, per_block), blocks, axis=0, mode=...]
    ppermute x3 -> x0, starting transfers between devices: 7.44 us -> none  [body(): lax.ppermute(send, 'frames', [(i, i ^ 1 << level) for i in range(size)])]
  transfers between devices with their start and end apart: 7 -> 0, of which waited for: 7 -> 0; matrix products, arithmetic and copies ran while one was open for 1% -> 0% of each run, Pallas kernels for 0% -> 0%
where the time goes in v3:
time: 170 us
  Pallas kernels  155 us (91%)
  matrix products  8.74 us (5%)
  local copies, waits for them, and re-layouts  2.96 us (2%)
  other arithmetic  2.11 us (1%)
    pallas_call x1, Pallas kernels, make_sketch(): pl.pallas_call(lambda *refs: sketch_kernel(scale, *refs), out_shape=(jax....  65.6 us
    pallas_call x2, Pallas kernels, sum_frames(): pl.pallas_call(frames_kernel, out_shape=(jax.ShapeDtypeStruct((2 * gram_h...  55.9 us
    pallas_call x2, Pallas kernels, sum_bins(): pl.pallas_call(lambda *refs: bins_kernel(count, *refs), out_shape=tuple((...  33.9 us

profile of v3, /device:TPU:0, one launch (start us, length us, event | category | flops | bytes accessed | tf_op | source)
XLA Modules:
  0.0 170.1 jit_solution(18110014292193263029)
XLA Ops:
  0.7 0.9 reshape.18
  1.6 0.6 gather_fusion
  2.1 0.1 copy.9
  2.2 1.1 convert_multiply_fusion
  3.4 0.5 fusion.20.refs_3_
  3.9 65.6 %make_sketch.1 = (f32[512,256]{1,0:T(8,128)S(1)}, f32[384,384]{1,0:T(8,128)S(1)}) custom-call(f32[2048,256]{1,0:T(8,128)S(1)} %copy-done, s32[1,2048]{1,0:T(1,128)S(1)} %bitcast.23, s32[512,8]{1,0:T(8,128)S(1)} %bitcast.22, f32[384,384]{1,0:T(8,128)S(1)} %fusion.20.refs_3_), custom_call_target="tpu_custom_call" | custom-call | tf_op jit(solution)/shard_map/make_sketch/pallas_call | solution.py:225
  69.5 0.6 fusion.18.refs_0_
  70.1 14.3 %sum_proj.1 = f32[512,384]{1,0:T(8,128)S(1)} custom-call(f32[512,384]{1,0:T(8,128)S(1)} %fusion.18.refs_0_), custom_call_target="tpu_custom_call" | custom-call | tf_op jit(solution)/shard_map/sum_proj/pallas_call | solution.py:290
  84.5 0.3 copy.8
  84.7 1.2 fusion.7
  85.9 0.8 fusion.15.g_ref
  86.8 0.8 fusion.32.c_ref
  87.6 26.9 %sum_frames.2 = (f32[384,384]{1,0:T(8,128)S(1)}, f32[384,256]{1,0:T(8,128)S(1)}) custom-call(f32[192,384]{1,0:T(8,128)S(1)} %fusion.15.g_ref, f32[384,256]{1,0:T(8,128)S(1)} %fusion.32.c_ref), custom_call_target="tpu_custom_call" | custom-call | tf_op jit(solution)/shard_map/sum_frames/pallas_call | solution.py:363
  114.4 0.6 fusion.11
  115.0 0.5 fusion.33.refs_0_
  115.5 0.6 fusion.34.refs_1_
  116.1 19.6 %sum_both.1 = (f32[384,384]{1,0:T(8,128)S(1)}, f32[512,384]{1,0:T(8,128)S(1)}) custom-call(f32[384,384]{1,0:T(8,128)S(1)} %fusion.33.refs_0_, f32[512,384]{1,0:T(8,128)S(1)} %fusion.34.refs_1_), custom_call_target="tpu_custom_call" | custom-call | tf_op jit(solution)/shard_map/sum_both/pallas_call | solution.py:290
  135.7 1.2 fusion.3
  136.9 0.8 fusion.35.c_ref
  137.7 0.8 fusion.13.g_ref
  138.5 29.1 %sum_frames.3 = (f32[384,384]{1,0:T(8,128)S(1)}, f32[384,256]{1,0:T(8,128)S(1)}) custom-call(f32[192,384]{1,0:T(8,128)S(1)} %fusion.13.g_ref, f32[384,256]{1,0:T(8,128)S(1)} %fusion.35.c_ref), custom_call_target="tpu_custom_call" | custom-call | tf_op jit(solution)/shard_map/sum_frames/pallas_call | solution.py:363
  167.6 0.5 fusion.36
  168.1 0.9 slice_multiply_fusion
  169.0 1.1 copy.12
  (13 shorter events, 0.1 us)
Async XLA Ops:
  0.6 3.3 %copy-start.1 = (s32[2048]{0:T(1024)S(1)}, s32[2048]{0:T(1024)}, u32[]{:S(2)}) copy-start(s32[2048]{0:T(1024)} %param.7) | copy-start | bytes 24580
  0.6 3.3 %copy-start = (f32[2048,256]{1,0:T(8,128)S(1)}, f32[2048,256]{1,0:T(8,128)}, u32[]{:S(2)}) copy-start(f32[2048,256]{1,0:T(8,128)} %refs_0_.1) | copy-start | bytes 6291460
  3.4 66.7 %copy-start.2 = (f32[352,256]{1,0:T(8,128)}, f32[352,256]{1,0:T(8,128)S(1)}, u32[]{:S(2)}) copy-start(f32[352,256]{1,0:T(8,128)S(1)} %convert_multiply_fusion) | copy-start | bytes 1081348
  69.5 14.9 %copy-start.4 = (f32[512,352]{0,1:T(8,128)S(1)}, f32[512,352]{0,1:T(8,128)}, u32[]{:S(2)}) copy-start(f32[512,352]{0,1:T(8,128)} %param.10) | copy-start | bytes 2162692
  85.9 28.5 %copy-start.3 = (f32[352,256]{1,0:T(8,128)S(1)}, f32[352,256]{1,0:T(8,128)}, u32[]{:S(2)}) copy-start(f32[352,256]{1,0:T(8,128)} %copy-done.2) | copy-start | bytes 1081348

commit v4 on v3

--- a/solution.py
+++ b/solution.py
@@ -135,8 +135,9 @@
 
 
 def sketch_kernel(
-    scale, x_ref, s_ref, k_ref, g_ref, out_ref, g_out,
-    term, high, low, rows_ref, got_y, got_z, part, g_core, g_sum, g_chip, send_sem, recv_sem,
+    scale, x_ref, s_ref, k_ref, g_ref, t_ref, out_ref, g_out, p_out,
+    term, high, low, rows_ref, got_y, got_z, part, g_core, g_sum, g_chip,
+    proj, p_core, p_sum, p_chip, send_sem, recv_sem,
 ):
     me, col = lax.axis_index("frames"), lax.axis_index("bins")
     core = lax.rem(col, 2)
@@ -147,23 +148,26 @@
     across = (me, flip(col, 2))
     greet([side, near, far, sibling, across])
     half = g_ref.shape[0] // 2
-    gram_1 = send(piece(g_ref, 1 - core, half), g_core, send_sem.at[7], recv_sem.at[7], sibling)
+    gram_1 = send(piece(g_ref, 1 - core, half), g_core, send_sem.at[14], recv_sem.at[14], sibling)
     frame_rows = x_ref.shape[0]
     outer = frame_rows // SIDE
     tile = 128
+    span = k_ref.shape[0] // 2
+    share = span // 2
+    spans = [pl.ds(0, span), pl.ds(span, span)]
     value = x_ref[...]
     rounded = value.astype(jnp.bfloat16)
     high[...] = rounded
     low[...] = (value - rounded.astype(jnp.float32)).astype(jnp.bfloat16)
 
-    def compute(r):
+    def compute(r, h):
         odd = 0
         for bit in range(3):
             if not r >> bit & 1:
                 odd = odd + lax.rem(me // (1 << bit), 2)
 
         def step(index, carry):
-            where = pl.ds(pl.multiple_of(index * tile, tile), tile)
+            where = pl.ds(pl.multiple_of(h * span + index * tile, tile), tile)
             kept = k_ref[where, r : r + 1]
             lane = lax.broadcasted_iota(jnp.int32, (tile, SIDE), 1)
             bits = fold(jnp.bitwise_and(kept, lane), SIDE.bit_length() - 1)
@@ -180,53 +184,114 @@
             )
             return carry
 
-        lax.fori_loop(0, k_ref.shape[0] // tile, step, 0)
-
-    copies = {}
-    for z in (3, 2, 1, 0):
-        compute(2 * z + 1)
-        copies[z] = send(term.at[2 * z + 1], got_y.at[z], send_sem.at[z], recv_sem.at[z], side)
-        if z == 3:
-            gram_1.wait_recv()
-            g_sum[...] = piece(g_ref, core, half)[...] + g_core[...]
-            gram_2 = send(g_sum, g_chip, send_sem.at[8], recv_sem.at[8], across)
-    compute(6)
-    copies[3].wait_recv()
-    part[0] = term[6] + got_y[3]
-    first = send(part.at[0], got_z.at[0], send_sem.at[4], recv_sem.at[4], near)
-    compute(4)
+        lax.fori_loop(0, span // tile, step, 0)
+
+    copies = []
+
+    def go(src, dst, n, device):
+        copies.append(send(src, dst, send_sem.at[n], recv_sem.at[n], device))
+        return copies[-1]
+
+    by_y, first, second, third, proj_1, proj_2, proj_3 = ({} for _ in range(7))
+
+    def odd_terms(h):
+        for z in (3, 2, 1, 0):
+            compute(2 * z + 1, h)
+            by_y[h, z] = go(term.at[2 * z + 1, spans[h]], got_y.at[z, spans[h]], 4 * h + z, side)
+
+    def to_near(h):
+        by_y[h, 3].wait_recv()
+        part[0, spans[h]] = term[6, spans[h]] + got_y[3, spans[h]]
+        first[h] = go(part.at[0, spans[h]], got_z.at[0, spans[h]], 8 + 3 * h, near)
+
+    def to_far(h):
+        by_y[h, 2].wait_recv()
+        first[h].wait_recv()
+        part[1, spans[h]] = term[4, spans[h]] + got_y[2, spans[h]] + got_z[0, spans[h]]
+        second[h] = go(part.at[1, spans[h]], got_z.at[1, spans[h]], 9 + 3 * h, far)
+
+    def last_near(h):
+        by_y[h, 1].wait_recv()
+        part[2, spans[h]] = term[2, spans[h]] + got_y[1, spans[h]]
+        third[h] = go(part.at[2, spans[h]], got_z.at[2, spans[h]], 10 + 3 * h, near)
+
+    def split(value):
+        top = value.astype(jnp.bfloat16)
+        return top, (value - top.astype(jnp.float32)).astype(jnp.bfloat16)
+
+    def finish(h):
+        here = spans[h]
+        by_y[h, 0].wait_recv()
+        third[h].wait_recv()
+        second[h].wait_recv()
+        sketch = ((term[0, here] + got_y[0, here]) + (got_z[2, here] + got_z[1, here])) * scale
+        out_ref[here] = sketch
+        s_high, s_low = split(sketch)
+        t_high, t_low = split(t_ref[...])
+
+        def dot(left, right):
+            return lax.dot_general(left, right, (((1,), (1,)), ((), ())), preferred_element_type=jnp.float32)
+
+        proj[here] = dot(s_high, t_high) + (dot(s_high, t_low) + dot(s_low, t_high))
+        theirs = piece(proj, 1 - core, share, h * span)
+        proj_1[h] = go(theirs, p_core.at[h], 17 + 3 * h, sibling)
+
+    def proj_across(h):
+        proj_1[h].wait_recv()
+        p_sum[h] = piece(proj, core, share, h * span)[...] + p_core[h]
+        proj_2[h] = go(p_sum.at[h], p_chip.at[h], 18 + 3 * h, across)
+
+    def proj_back(h):
+        proj_2[h].wait_recv()
+        mine = piece(p_out, core, share, h * span)
+        mine[...] = p_sum[h] + p_chip[h]
+        proj_3[h] = go(mine, mine, 19 + 3 * h, sibling)
+
+    odd_terms(0)
+    gram_1.wait_recv()
+    g_sum[...] = piece(g_ref, core, half)[...] + g_core[...]
+    gram_2 = go(g_sum, g_chip, 15, across)
+    compute(6, 0)
+    to_near(0)
+    compute(4, 0)
+    odd_terms(1)
+    to_far(0)
+    compute(2, 0)
+    compute(0, 0)
+    last_near(0)
     gram_2.wait_recv()
     mine = piece(g_out, core, half)
     mine[...] = g_sum[...] + g_chip[...]
-    gram_3 = send(mine, mine, send_sem.at[9], recv_sem.at[9], sibling)
-    compute(2)
-    copies[2].wait_recv()
-    first.wait_recv()
-    part[1] = term[4] + got_y[2] + got_z[0]
-    second = send(part.at[1], got_z.at[1], send_sem.at[5], recv_sem.at[5], far)
-    compute(0)
-    copies[1].wait_recv()
-    part[2] = term[2] + got_y[1]
-    third = send(part.at[2], got_z.at[2], send_sem.at[6], recv_sem.at[6], near)
-    copies[0].wait_recv()
-    third.wait_recv()
-    second.wait_recv()
-    out_ref[...] = ((term[0] + got_y[0]) + (got_z[2] + got_z[1])) * scale
+    gram_3 = go(mine, mine, 16, sibling)
+    for r in (6, 4, 2, 0):
+        compute(r, 1)
+    finish(0)
+    to_near(1)
+    proj_across(0)
+    to_far(1)
+    proj_back(0)
+    last_near(1)
+    finish(1)
+    proj_across(1)
+    proj_back(1)
     gram_3.wait_recv()
-    for copy in (*copies.values(), first, second, third, gram_1, gram_2, gram_3):
+    for h in (0, 1):
+        proj_3[h].wait_recv()
+    for copy in (gram_1, *copies):
         copy.wait_send()
 
 
-def make_sketch(spectrum, sign_row, kept, gram, scale):
+def make_sketch(spectrum, sign_row, kept, gram, templates, scale):
     frame_rows, cols = spectrum.shape
     rows = kept.shape[0]
+    parts = templates.shape[0]
     half = (gram.shape[0] // 2, gram.shape[1])
     f32, bf16 = jnp.float32, jnp.bfloat16
     return pl.pallas_call(
         lambda *refs: sketch_kernel(scale, *refs),
-        out_shape=(jax.ShapeDtypeStruct((rows, cols), f32), jax.ShapeDtypeStruct(gram.shape, f32)),
-        in_specs=[VMEM] * 4,
-        out_specs=(VMEM, VMEM),
+        out_shape=(jax.ShapeDtypeStruct((rows, cols), f32), jax.ShapeDtypeStruct(gram.shape, f32), jax.ShapeDtypeStruct((rows, parts), f32)),
+        in_specs=[VMEM] * 5,
+        out_specs=(VMEM, VMEM, VMEM),
         scratch_shapes=[
             pltpu.VMEM((8, rows, cols), f32),
             pltpu.VMEM((frame_rows, cols), bf16),
@@ -238,12 +303,16 @@
             pltpu.VMEM(half, f32),
             pltpu.VMEM(half, f32),
             pltpu.VMEM(half, f32),
-            DMA((10,)),
-            DMA((10,)),
+            pltpu.VMEM((rows, parts), f32),
+            pltpu.VMEM((2, rows // 4, parts), f32),
+            pltpu.VMEM((2, rows // 4, parts), f32),
+            pltpu.VMEM((2, rows // 4, parts), f32),
+            DMA((23,)),
+            DMA((23,)),
         ],
         compiler_params=pltpu.CompilerParams(collective_id=0, has_side_effects=True, vmem_limit_bytes=LIMIT),
         name="make_sketch",
-    )(spectrum, sign_row, kept, gram)
+    )(spectrum, sign_row, kept, gram, templates)
 
 
 def bins_kernel(count, *refs):
@@ -389,20 +458,23 @@
     activations = jnp.pad(w_init, ((0, 0), (0, padded - parts)))
     blocks = jnp.bitwise_xor(position, jnp.arange(block_count, dtype=jnp.int32))
     kept = jnp.take(kept_rows.reshape(block_count, per_block), blocks, axis=0, mode="clip").T
-    sketch, gram_h = make_sketch(
+    sketch, gram_h, proj = make_sketch(
         spectrum,
         sign_bits.reshape(1, frame_rows),
         kept,
         jnp.dot(templates, templates.T, precision=high),
+        templates,
         1.0 / (frame_rows * block_count) ** 0.5,
     )
     half = padded // 2
     for round_index in range(ITERS):
-        proj = jnp.dot(sketch, templates.T, precision=high)
-        if round_index == 0:
-            (proj,) = sum_bins("sum_proj", 1, proj)
-        else:
-            gram_h, proj = sum_bins("sum_both", 3, jnp.dot(templates, templates.T, precision=high), proj)
+        if round_index:
+            gram_h, proj = sum_bins(
+                "sum_bins",
+                1,
+                jnp.dot(templates, templates.T, precision=high),
+                jnp.dot(sketch, templates.T, precision=high),
+            )
         lower = jnp.maximum(-proj, 0.0) + jnp.dot(activations, gram_h, precision=high) + damping
         activations = activations * jnp.sqrt((jnp.maximum(proj, 0.0) + damping) / lower)
         own = lax.dynamic_slice_in_dim(activations, core * half, half, axis=1)

time: 170 us -> 160 us (0.941)
  Pallas kernels: 155 us -> 143 us
  local copies, waits for them, and re-layouts: 2.96 us -> 4.96 us
    pallas_call x2 -> x1, Pallas kernels: 33.9 us -> 19.6 us  [sum_bins(): pl.pallas_call(lambda *refs: bins_kernel(count, *refs), out_shape=tuple((...]
    unnamed x12, local copies, waits for them, and re-layouts: 1.41 us -> 3.39 us
    pallas_call x1, Pallas kernels: 65.6 us -> 67.4 us  [make_sketch(): pl.pallas_call(lambda *refs: sketch_kernel(scale, *refs), out_shape=(jax....]
where the time goes in v4:
time: 160 us
  Pallas kernels  143 us (89%)
  matrix products  9.35 us (6%)
  local copies, waits for them, and re-layouts  4.96 us (3%)
  other arithmetic  2.11 us (1%)
    pallas_call x1, Pallas kernels, make_sketch(): pl.pallas_call(lambda *refs: sketch_kernel(scale, *refs), out_shape=(jax....  67.4 us
    pallas_call x2, Pallas kernels, sum_frames(): pl.pallas_call(frames_kernel, out_shape=(jax.ShapeDtypeStruct((2 * gram_h...  55.6 us
    pallas_call x1, Pallas kernels, sum_bins(): pl.pallas_call(lambda *refs: bins_kernel(count, *refs), out_shape=tuple((...  19.6 us
    dot_general x2, matrix products, body_8x4(): jnp.dot(activations, gram_h, precision=high)  3.51 us
    unnamed x12, local copies, waits for them, and re-layouts  3.39 us

profile of v4, /device:TPU:0, one launch (start us, length us, event | category | flops | bytes accessed | tf_op | source)
XLA Modules:
  0.0 159.9 jit_solution(16235794077479250577)
XLA Ops:
  0.7 0.9 reshape.18
  1.6 0.6 gather_fusion
  2.1 0.1 copy.9
  2.2 1.1 convert_multiply_fusion
  3.4 0.0 copy-start.3
  3.4 0.5 fusion.25.refs_3_
  3.9 67.4 %make_sketch.1 = (f32[512,256]{1,0:T(8,128)S(1)}, f32[384,384]{1,0:T(8,128)S(1)}, f32[512,384]{1,0:T(8,128)S(1)}) custom-call(f32[2048,256]{1,0:T(8,128)S(1)} %copy-done, s32[1,2048]{1,0:T(1,128)S(1)} %bitcast.22, s32[512,8]{1,0:T(8,128)S(1)} %bitcast.21, f32[384,384]{1,0:T(8,128)S(1)} %fusion.25.refs_3_, f32[384,256]{1,0:T(8,128)S(1)} %pad.9.refs_4_), custom_call_target="tpu_custom_call" | custom-call | tf_op jit(solution)/shard_map/make_sketch/pallas_call | solution.py:290
  71.4 0.9 copy-done.2
  72.3 1.4 copy.8
  73.7 2.3 %fusion.7 = f32[512,384]{1,0:T(8,128)S(1)} fusion(f32[384,384]{1,0:T(8,128)S(1)} %get-tuple-element.12, f32[512,384]{1,0:T(8,128)} %copy-done.2, f32[512,352]{1,0:T(8,128)S(1)} %copy.8), kind=kOutput, calls=%fused_computation.10 | convolution fusion | flops 454557696 | bytes 2883584 | tf_op jit(solution)/shard_map/dot_general | solution.py:478
  76.0 0.8 fusion.15.g_ref
  76.8 0.8 fusion.29.c_ref
  77.7 26.4 %sum_frames.2 = (f32[384,384]{1,0:T(8,128)S(1)}, f32[384,256]{1,0:T(8,128)S(1)}) custom-call(f32[192,384]{1,0:T(8,128)S(1)} %fusion.15.g_ref, f32[384,256]{1,0:T(8,128)S(1)} %fusion.29.c_ref), custom_call_target="tpu_custom_call" | custom-call | tf_op jit(solution)/shard_map/sum_frames/pallas_call | solution.py:432
  104.1 0.6 fusion.11
  104.7 0.5 fusion.30.refs_0_
  105.2 0.6 fusion.31.refs_1_
  105.8 19.6 %sum_bins.1 = (f32[384,384]{1,0:T(8,128)S(1)}, f32[512,384]{1,0:T(8,128)S(1)}) custom-call(f32[384,384]{1,0:T(8,128)S(1)} %fusion.30.refs_0_, f32[512,384]{1,0:T(8,128)S(1)} %fusion.31.refs_1_), custom_call_target="tpu_custom_call" | custom-call | tf_op jit(solution)/shard_map/sum_bins/pallas_call | solution.py:359
  125.4 1.2 fusion.3
  126.5 0.8 fusion.32.c_ref
  127.4 0.8 fusion.13.g_ref
  128.2 29.1 %sum_frames.3 = (f32[384,384]{1,0:T(8,128)S(1)}, f32[384,256]{1,0:T(8,128)S(1)}) custom-call(f32[192,384]{1,0:T(8,128)S(1)} %fusion.13.g_ref, f32[384,256]{1,0:T(8,128)S(1)} %fusion.32.c_ref), custom_call_target="tpu_custom_call" | custom-call | tf_op jit(solution)/shard_map/sum_frames/pallas_call | solution.py:432
  157.3 0.5 fusion.33
  157.8 0.9 slice_multiply_fusion
  158.7 1.1 copy.12
  (12 shorter events, 0.1 us)
Async XLA Ops:
  0.6 3.3 %copy-start.1 = (s32[2048]{0:T(1024)S(1)}, s32[2048]{0:T(1024)}, u32[]{:S(2)}) copy-start(s32[2048]{0:T(1024)} %param.7) | copy-start | bytes 24580
  0.6 3.3 %copy-start = (f32[2048,256]{1,0:T(8,128)S(1)}, f32[2048,256]{1,0:T(8,128)}, u32[]{:S(2)}) copy-start(f32[2048,256]{1,0:T(8,128)} %refs_0_.1) | copy-start | bytes 6291460
  3.4 68.0 %copy-start.3 = (f32[352,256]{1,0:T(8,128)}, f32[352,256]{1,0:T(8,128)S(1)}, u32[]{:S(2)}) copy-start(f32[352,256]{1,0:T(8,128)S(1)} %convert_multiply_fusion) | copy-start | bytes 1081348
  71.4 0.9 copy-start.2
  76.0 28.1 %copy-start.4 = (f32[352,256]{1,0:T(8,128)S(1)}, f32[352,256]{1,0:T(8,128)}, u32[]{:S(2)}) copy-start(f32[352,256]{1,0:T(8,128)} %copy-done.3) | copy-start | bytes 1081348

commit v5 on v4

--- a/solution.py
+++ b/solution.py
@@ -367,16 +367,36 @@
     )(*arrays)
 
 
-def frames_kernel(g_ref, c_ref, g_out, c_out, g_y, c_y, g_z, c_z, g_part, c_part, send_sem, recv_sem):
+def pack(gram, packed):
+    n = packed.shape[0] // 2
+    packed[:n] = gram[:n]
+    packed[n:, : 2 * n] = gram[n : 2 * n, n:]
+    packed[n:, 2 * n :] = gram[2 * n :, 2 * n :]
+
+
+def unpack(packed, gram):
+    n = packed.shape[0] // 2
+    gram[:n] = packed[:n]
+    gram[n : 2 * n, :n] = packed[:n, n : 2 * n].T
+    gram[2 * n :, :n] = packed[:n, 2 * n :].T
+    gram[n : 2 * n, n:] = packed[n:, : 2 * n]
+    gram[2 * n :, n : 2 * n] = packed[n:, n : 2 * n].T
+    gram[2 * n :, 2 * n :] = packed[n:, 2 * n :]
+
+
+def frames_kernel(
+    g_ref, c_ref, g_full, c_out, g_y, c_y, g_z, c_z, g_part, c_part, g_in, g_out, send_sem, recv_sem
+):
     me, col = lax.axis_index("frames"), lax.axis_index("bins")
     core = lax.rem(col, 2)
     side = (flip(me, 1), col)
     peers = {z: (flip(me, 2 * z), col) for z in (3, 2, 1)}
     sibling = (me, flip(col, 1))
+    pack(g_ref, g_in)
     greet([side, *peers.values(), sibling])
-    g_half = g_ref.shape[0]
+    g_half = g_in.shape[0] // 2
     arrays = (
-        (0, g_ref, g_half // 8, g_y, g_z, g_part, g_out, core * g_half),
+        (0, g_in.at[pl.ds(pl.multiple_of(core * g_half, 8), g_half)], g_half // 8, g_y, g_z, g_part, g_out, core * g_half),
         (16, c_ref, c_ref.shape[0] // 8, c_y, c_z, c_part, c_out, 0),
     )
     copies = []
@@ -420,28 +440,30 @@
     for z in (1, 2, 3):
         passed[16, z].wait_recv()
     swap.wait_recv()
+    unpack(g_out, g_full)
     for copy in copies:
         copy.wait_send()
 
 
-def sum_frames(gram_half, cross):
+def sum_frames(gram, cross):
     f32 = jnp.float32
     parts, cols = cross.shape
-    g_piece = (gram_half.shape[0] // 8, gram_half.shape[1])
+    packed = (2 * gram.shape[0] // 3, gram.shape[1])
+    g_piece = (packed[0] // 16, packed[1])
     c_piece = (parts // 8, cols)
     return pl.pallas_call(
         frames_kernel,
         out_shape=(
-            jax.ShapeDtypeStruct((2 * gram_half.shape[0], gram_half.shape[1]), f32),
+            jax.ShapeDtypeStruct(gram.shape, f32),
             jax.ShapeDtypeStruct(cross.shape, f32),
         ),
         in_specs=[VMEM, VMEM],
         out_specs=(VMEM, VMEM),
         scratch_shapes=[pltpu.VMEM((count, *shape), f32) for count in (4, 3, 3) for shape in (g_piece, c_piece)]
-        + [DMA((32,)), DMA((32,))],
+        + [pltpu.VMEM(packed, f32), pltpu.VMEM(packed, f32), DMA((32,)), DMA((32,))],
         compiler_params=pltpu.CompilerParams(collective_id=2, has_side_effects=True, vmem_limit_bytes=LIMIT),
         name="sum_frames",
-    )(gram_half, cross)
+    )(gram, cross)
 
 
 def body_8x4(spectrum, sign_bits, kept_rows, mask, w_init, h_init):
@@ -449,7 +471,6 @@
     high = lax.Precision.HIGH
     block_count = 8
     position = lax.axis_index("frames")
-    core = lax.rem(lax.axis_index("bins"), 2)
     frame_rows, cols = spectrum.shape
     per_block = kept_rows.shape[0] // block_count
     parts = w_init.shape[1]
@@ -466,7 +487,6 @@
         templates,
         1.0 / (frame_rows * block_count) ** 0.5,
     )
-    half = padded // 2
     for round_index in range(ITERS):
         if round_index:
             gram_h, proj = sum_bins(
@@ -477,9 +497,8 @@
             )
         lower = jnp.maximum(-proj, 0.0) + jnp.dot(activations, gram_h, precision=high) + damping
         activations = activations * jnp.sqrt((jnp.maximum(proj, 0.0) + damping) / lower)
-        own = lax.dynamic_slice_in_dim(activations, core * half, half, axis=1)
         gram_w, cross = sum_frames(
-            jnp.dot(own.T, activations, precision=high),
+            jnp.dot(activations.T, activations, precision=high),
             jnp.dot(activations.T, sketch, precision=high),
         )
         lower = jnp.maximum(-cross, 0.0) + jnp.dot(gram_w, templates, precision=high) + damping

time: 160 us -> 155 us (0.969)
  Pallas kernels: 143 us -> 138 us
    pallas_call x2, Pallas kernels: 55.6 us -> 50.6 us  [sum_frames(): pl.pallas_call(frames_kernel, out_shape=(jax.ShapeDtypeStruct(gram.shape,...]
where the time goes in v5:
time: 155 us
  Pallas kernels  138 us (89%)
  matrix products  9.33 us (6%)
  local copies, waits for them, and re-layouts  4.97 us (3%)
  other arithmetic  2.11 us (1%)
    pallas_call x1, Pallas kernels, make_sketch(): pl.pallas_call(lambda *refs: sketch_kernel(scale, *refs), out_shape=(jax....  67.4 us
    pallas_call x2, Pallas kernels, sum_frames(): pl.pallas_call(frames_kernel, out_shape=(jax.ShapeDtypeStruct(gram.shape,...  50.6 us
    pallas_call x1, Pallas kernels, sum_bins(): pl.pallas_call(lambda *refs: bins_kernel(count, *refs), out_shape=tuple((...  19.6 us
    dot_general x2, matrix products, body_8x4(): jnp.dot(activations, gram_h, precision=high)  3.5 us
    unnamed x12, local copies, waits for them, and re-layouts  3.39 us

profile of v5, /device:TPU:0, one launch (start us, length us, event | category | flops | bytes accessed | tf_op | source)
XLA Modules:
  0.0 154.8 jit_solution(311729243408324459)
XLA Ops:
  0.7 0.9 reshape.18
  1.5 0.6 gather_fusion
  2.1 0.1 copy.9
  2.2 1.1 convert_multiply_fusion
  3.4 0.0 copy-start.3
  3.4 0.5 fusion.19.refs_3_
  3.9 67.4 %make_sketch.1 = (f32[512,256]{1,0:T(8,128)S(1)}, f32[384,384]{1,0:T(8,128)S(1)}, f32[512,384]{1,0:T(8,128)S(1)}) custom-call(f32[2048,256]{1,0:T(8,128)S(1)} %copy-done, s32[1,2048]{1,0:T(1,128)S(1)} %bitcast.24, s32[512,8]{1,0:T(8,128)S(1)} %bitcast.23, f32[384,384]{1,0:T(8,128)S(1)} %fusion.19.refs_3_, f32[384,256]{1,0:T(8,128)S(1)} %pad.9.refs_4_), custom_call_target="tpu_custom_call" | custom-call | tf_op jit(solution)/shard_map/make_sketch/pallas_call | solution.py:290
  71.4 0.9 copy-done.2
  72.3 1.4 copy.8
  73.6 2.3 %fusion.7 = f32[512,384]{1,0:T(8,128)S(1)} fusion(f32[384,384]{1,0:T(8,128)S(1)} %get-tuple-element.12, f32[512,384]{1,0:T(8,128)} %copy-done.2, f32[512,352]{1,0:T(8,128)S(1)} %copy.8), kind=kOutput, calls=%fused_computation.10 | convolution fusion | flops 454557696 | bytes 2883584 | tf_op jit(solution)/shard_map/dot_general | solution.py:498
  76.0 0.8 fusion.24.c_ref
  76.8 0.8 fusion.23.g_ref
  77.6 24.8 %sum_frames.2 = (f32[384,384]{1,0:T(8,128)S(1)}, f32[384,256]{1,0:T(8,128)S(1)}) custom-call(f32[384,384]{1,0:T(8,128)S(1)} %fusion.23.g_ref, f32[384,256]{1,0:T(8,128)S(1)} %fusion.24.c_ref), custom_call_target="tpu_custom_call" | custom-call | tf_op jit(solution)/shard_map/sum_frames/pallas_call | solution.py:454
  102.5 0.6 fusion.11
  103.1 0.5 fusion.25.refs_0_
  103.6 0.6 fusion.26.refs_1_
  104.1 19.6 %sum_bins.1 = (f32[384,384]{1,0:T(8,128)S(1)}, f32[512,384]{1,0:T(8,128)S(1)}) custom-call(f32[384,384]{1,0:T(8,128)S(1)} %fusion.25.refs_0_, f32[512,384]{1,0:T(8,128)S(1)} %fusion.26.refs_1_), custom_call_target="tpu_custom_call" | custom-call | tf_op jit(solution)/shard_map/sum_bins/pallas_call | solution.py:359
  123.7 1.2 fusion.3
  124.9 0.8 fusion.28.c_ref
  125.7 0.8 fusion.27.g_ref
  126.5 25.7 %sum_frames.3 = (f32[384,384]{1,0:T(8,128)S(1)}, f32[384,256]{1,0:T(8,128)S(1)}) custom-call(f32[384,384]{1,0:T(8,128)S(1)} %fusion.27.g_ref, f32[384,256]{1,0:T(8,128)S(1)} %fusion.28.c_ref), custom_call_target="tpu_custom_call" | custom-call | tf_op jit(solution)/shard_map/sum_frames/pallas_call | solution.py:454
  152.3 0.5 fusion.29
  152.8 0.9 slice_multiply_fusion
  153.7 1.1 copy.12
  (12 shorter events, 0.1 us)
Async XLA Ops:
  0.6 3.3 %copy-start.1 = (s32[2048]{0:T(1024)S(1)}, s32[2048]{0:T(1024)}, u32[]{:S(2)}) copy-start(s32[2048]{0:T(1024)} %param.7) | copy-start | bytes 24580
  0.6 3.3 %copy-start = (f32[2048,256]{1,0:T(8,128)S(1)}, f32[2048,256]{1,0:T(8,128)}, u32[]{:S(2)}) copy-start(f32[2048,256]{1,0:T(8,128)} %refs_0_.1) | copy-start | bytes 6291460
  3.4 68.0 %copy-start.3 = (f32[352,256]{1,0:T(8,128)}, f32[352,256]{1,0:T(8,128)S(1)}, u32[]{:S(2)}) copy-start(f32[352,256]{1,0:T(8,128)S(1)} %convert_multiply_fusion) | copy-start | bytes 1081348
  71.4 0.9 copy-start.2
  76.0 26.5 %copy-start.4 = (f32[352,256]{1,0:T(8,128)S(1)}, f32[352,256]{1,0:T(8,128)}, u32[]{:S(2)}) copy-start(f32[352,256]{1,0:T(8,128)} %copy-done.3) | copy-start | bytes 1081348
